TPU v7x, 32 devices: a whole 2x2x4 slice. The times are simulated.
32 devices in a mesh: seg: 4 (over y, x), rank: 8 (over z, core).
Axes of the slice: x: 2, y: 2, z: 4, core: 2. Of those that a mesh axis runs over, the one named last changes fastest.
Arguments:
- parent_nodes: float32 [81920, 375], P(('seg', 'rank')), as said below
- marks: int32 [32, 256], P(('seg', 'rank')), may hold values from 0 to 2559, as said below
- child_owner: int32 [65536, 1], P(('seg', 'rank')), may hold values from 0 to 31; in each aligned block of 2048 rows (0 to 2047, 2048 to 4095, ...) at most 128 rows name the same one
- face_link: int32 [131072, 6], P(('seg', 'rank')), may hold values from 0 to 12287
Outputs:
- node_mass: float32 [125, 131072], P(None, ('seg', 'rank'))
- face_mass: float32 [150, 131072], P(None, ('seg', 'rank'))
Inputs may be any that keep to these rules, and one draw needn't show every extreme that they name: `marks`: each row holds distinct local parent indices of its device. `child_owner`: among the children of one device no owner is named more than 128 times, a bound that some block reaches. `face_link`: the first 4096 values name slots of the previous owner along rank, the next 4096 own slots, the last 4096 slots of the next owner. `parent_nodes`: nodes of a slightly perturbed cube of side 3 to 6 around a point of the box from -8 to 8.
All inputs are finite; a program needn't handle non-finite values.
Results may differ from a plain program's by a relative error of at most 0.0003.
Values sent between devices are 32-bit elements; how exact they have to be, the bound alone decides.
A program may use at most 192 MiB of HBM per device.

v0:
```python
import math

import jax
import jax.numpy as jnp
import numpy as np
from jax import lax
from jax.sharding import PartitionSpec as P


def shifted(array, axis, by):
    count = lax.axis_size(axis)
    pairs = [(i, i + by) for i in range(count) if 0 <= i + by < count]
    return lax.ppermute(array, axis, pairs)


def gll_tables():
    points = np.array([-1.0, -math.sqrt(3.0 / 7.0), 0.0, math.sqrt(3.0 / 7.0), 1.0])
    weights = np.array([0.1, 49.0 / 90.0, 32.0 / 45.0, 49.0 / 90.0, 0.1])
    barycentric = np.array(
        [1.0 / np.prod([points[j] - points[m] for m in range(5) if m != j]) for j in range(5)]
    )
    slopes = np.zeros((5, 5))
    for i in range(5):
        for j in range(5):
            if i != j:
                slopes[i, j] = barycentric[j] / barycentric[i] / (points[i] - points[j])
        slopes[i, i] = -np.sum(slopes[i])

    def lagrange_at(where):
        table = np.ones((5, 5))
        for a in range(5):
            for j in range(5):
                for m in range(5):
                    if m != j:
                        table[a, j] *= (where[a] - points[m]) / (points[j] - points[m])
        return table

    def blend(value, side):
        return (1.0 - value) / 2.0 if side == 0 else (1.0 + value) / 2.0

    def flat(i, j, k):
        return i * 25 + j * 5 + k

    ends = (0, 4)
    gordon = np.zeros((125, 125))
    for i in range(5):
        for j in range(5):
            for k in range(5):
                r, s, t = (points[i], points[j], points[k])
                target = flat(i, j, k)
                for a in range(2):
                    gordon[target, flat(ends[a], j, k)] += blend(r, a)
                    gordon[target, flat(i, ends[a], k)] += blend(s, a)
                    gordon[target, flat(i, j, ends[a])] += blend(t, a)
                    for b in range(2):
                        gordon[target, flat(ends[a], ends[b], k)] -= blend(r, a) * blend(s, b)
                        gordon[target, flat(ends[a], j, ends[b])] -= blend(r, a) * blend(t, b)
                        gordon[target, flat(i, ends[a], ends[b])] -= blend(s, a) * blend(t, b)
                        for c in range(2):
                            gordon[target, flat(ends[a], ends[b], ends[c])] += (
                                blend(r, a) * blend(s, b) * blend(t, c)
                            )
    children = np.zeros((8, 125, 125))
    for octant in range(8):
        shifts = [2 * (octant >> 2 & 1) - 1, 2 * (octant >> 1 & 1) - 1, 2 * (octant & 1) - 1]
        tables = [lagrange_at((points + shifts[q]) / 2.0) for q in range(3)]
        children[octant] = np.kron(np.kron(tables[0], tables[1]), tables[2]) @ gordon
    identity = np.eye(5)
    derivs = [
        np.kron(np.kron(slopes, identity), identity),
        np.kron(np.kron(identity, slopes), identity),
        np.kron(np.kron(identity, identity), slopes),
    ]
    deriv_table = np.concatenate([derivs[q].T for q in range(3)], axis=1)
    mass_weights = np.kron(np.kron(weights, weights), weights)
    face_weights = np.kron(weights, weights)
    tangents = [(1, 2), (1, 2), (0, 2), (0, 2), (0, 1), (0, 1)]
    boundary = [
        flat(i, j, k)
        for i in range(5)
        for j in range(5)
        for k in range(5)
        if i in ends or j in ends or k in ends
    ]
    children_map = children.transpose(2, 0, 1).reshape(125, 1000)
    return (children_map, deriv_table, mass_weights, face_weights, tangents, np.array(boundary))


def geometry(coords, tables):
    children_map, deriv_table, mass_weights, face_weights, tangents, boundary = tables
    width = coords.shape[0]
    deriv = jnp.einsum(
        "wcn,nm->cmw",
        coords.reshape(width, 3, 125),
        jnp.asarray(deriv_table, jnp.float32),
        precision=lax.Precision.HIGHEST,
        preferred_element_type=jnp.float32,
    )
    deriv = deriv.reshape(3, 3, 5, 5, 5, width)
    jac = [[deriv[c, d] for d in range(3)] for c in range(3)]
    determinant = (
        jac[0][0] * (jac[1][1] * jac[2][2] - jac[1][2] * jac[2][1])
        - jac[0][1] * (jac[1][0] * jac[2][2] - jac[1][2] * jac[2][0])
        + jac[0][2] * (jac[1][0] * jac[2][1] - jac[1][1] * jac[2][0])
    )
    mass = determinant.reshape(125, width) * jnp.asarray(mass_weights, jnp.float32)[:, None]
    areas = []
    for face in range(6):
        first, second = tangents[face]
        direction = face // 2
        side = 0 if face % 2 == 0 else 4
        along = lax.index_in_dim(deriv[:, first], side, axis=1 + direction, keepdims=False)
        across = lax.index_in_dim(deriv[:, second], side, axis=1 + direction, keepdims=False)
        normal_x = along[1] * across[2] - along[2] * across[1]
        normal_y = along[2] * across[0] - along[0] * across[2]
        normal_z = along[0] * across[1] - along[1] * across[0]
        length = jnp.sqrt(normal_x * normal_x + normal_y * normal_y + normal_z * normal_z).reshape(
            25, width
        )
        areas.append(length * jnp.asarray(face_weights, jnp.float32)[:, None])
    return (mass, jnp.concatenate(areas, axis=0))


def blocked_geometry(coords_of, total, tables):
    width = 512
    blocks = total // width

    def run_block(number, carry):
        mass_all, faces_all = carry
        mass, faces = geometry(coords_of(number * width, width), tables)
        mass_all = lax.dynamic_update_slice_in_dim(mass_all, mass, number * width, 1)
        faces_all = lax.dynamic_update_slice_in_dim(faces_all, faces, number * width, 1)
        return (mass_all, faces_all)

    start = (jnp.zeros((125, total), jnp.float32), jnp.zeros((150, total), jnp.float32))
    return lax.fori_loop(0, blocks, run_block, start)


def body(parent_nodes, marks, child_owner, face_link):
    tables = gll_tables()
    children_map = jnp.asarray(tables[0], jnp.float32)
    seg_count = lax.axis_size("seg")
    rank_count = lax.axis_size("rank")
    devices = seg_count * rank_count
    kids = child_owner.shape[0]
    marked = marks.shape[1]
    capacity = max(2, 2 * kids // devices)
    slot_count = devices * capacity
    owners = child_owner[:, 0]
    onehot = (owners[:, None] == jnp.arange(devices, dtype=jnp.int32)[None, :]).astype(jnp.int32)
    position = jnp.sum(jnp.cumsum(onehot, axis=0) * onehot, axis=1) - 1
    target = owners * capacity + position
    picked = parent_nodes[marks[0]]
    made = jnp.dot(
        picked.reshape(marked * 3, 125),
        children_map,
        precision=lax.Precision.HIGHEST,
        preferred_element_type=jnp.float32,
    )
    made = made.reshape(marked, 3, 8, 125).transpose(0, 2, 1, 3).reshape(kids, 375)
    outgoing = jnp.zeros((slot_count, 375), jnp.float32).at[target].set(made)
    outgoing = outgoing.reshape(seg_count, rank_count, capacity, 375)
    arrived = lax.all_to_all(
        lax.all_to_all(outgoing, "seg", split_axis=0, concat_axis=0, tiled=True),
        "rank",
        split_axis=1,
        concat_axis=1,
        tiled=True,
    ).reshape(slot_count, 375)

    def coords_of(start, width):
        return lax.dynamic_slice_in_dim(arrived, start, width, 0)

    mass, faces = blocked_geometry(coords_of, slot_count, tables)
    before = shifted(faces, "rank", 1)
    after = shifted(faces, "rank", -1)
    pool = jnp.concatenate([before, faces, after], axis=1).reshape(6, 25, 3 * slot_count)
    fetched = []
    for face in range(6):
        opposite = face + 1 - 2 * (face % 2)
        fetched.append(jnp.take(pool[opposite], face_link[:, face], axis=1))
    return (mass, faces + jnp.concatenate(fetched, axis=0))


def solution(mesh):
    return jax.shard_map(
        body,
        mesh=mesh,
        in_specs=(
            P(("seg", "rank"), None),
            P(("seg", "rank"), None),
            P(("seg", "rank"), None),
            P(("seg", "rank"), None),
        ),
        out_specs=(P(None, ("seg", "rank")), P(None, ("seg", "rank"))),
        check_vma=False,
    )
```

profile of v0, /device:TPU:1, one launch (start us, length us, event | category | flops | bytes accessed | tf_op | source)
XLA Modules:
  0.0 636.7 jit_solution(1584573100240405385)
XLA Ops:
  1.3 9.1 %reduce-window.6 = s32[32,16,128]{2,1,0:T(8,128)S(1)} reduce-window(s32[32,16,128]{2,1,0:T(8,128)S(1)} %fusion.7, s32[]{:T(128)} %constant.61.clone.1), window={size=1x1x128 pad=0_0x0_0x127_0}, to_apply=%region_0.0 | reduce-window | flops 8323072 | bytes 524292 | tf_op jit(solution)/shard_map/reduce-window
  12.7 5.5 copy.74
  18.2 3.3 gather_fusion
  24.5 4.1 copy.77
  28.6 4.6 reshape.510
  33.2 12.1 %scatter_custom_fusion = f32[4096,375]{1,0:T(8,128)} fusion(s32[2048]{0:T(1024)S(1)} %bitcast.94, f32[2048,375]{1,0:T(8,128)S(1)} %reshape.510, f32[]{:T(128)} %constant.62.clone.1), kind=kCustom, calls=%fused_computation.33 | custom fusion | bytes 6144004 | tf_op jit(solution)/shard_map/scatter | solution.py:161
  45.3 6.6 %copy.78 = f32[4,8,128,375]{2,1,3,0:T(8,128)} copy(f32[4,8,128,375]{3,2,1,0:T(8,128)} %bitcast.73) | data formatting | bytes 12288000 | tf_op jit(solution)/shard_map/reshape | solution.py:162
  51.9 72.9 %all_to_all.10 = f32[4,8,128,375]{2,1,3,0:T(8,128)S(1)} all-to-all(f32[4,8,128,375]{2,1,3,0:T(8,128)} %copy.78), channel_id=1, replica_groups=mesh['seg'=4,'rank'=8] {'seg'}, dimensions={0} | all-to-all | bytes 12288000 | tf_op jit(solution)/shard_map/all_to_all | solution.py:164
  124.8 4.2 copy.79
  129.0 6.6 %all-to-all-start.1 = ((f32[4,8,128,375]{2,0,3,1:T(4,128)}), f32[4,8,128,375]{2,0,3,1:T(4,128)}, u32[]{:S(2)}, u32[]{:S(2)}) async-start(f32[4,8,128,375]{2,0,3,1:T(4,128)} %copy.79), calls=%async_computation.1 | async-start | bytes 12288000 | tf_op jit(solution)/shard_map/all_to_all | solution.py:163
  135.7 134.9 %all-to-all-done.1 = f32[4,8,128,375]{2,0,3,1:T(4,128)} async-done(((f32[4,8,128,375]{2,0,3,1:T(4,128)}), f32[4,8,128,375]{2,0,3,1:T(4,128)}, u32[]{:S(2)}, u32[]{:S(2)}) %all-to-all-start.1) | async-done | bytes 6144032 | tf_op jit(solution)/shard_map/all_to_all | solution.py:163
  270.7 7.7 %copy.80 = f32[4,8,128,375]{3,2,1,0:T(8,128)} copy(f32[4,8,128,375]{2,0,3,1:T(4,128)} %all-to-all-done.1) | data formatting | bytes 12288000 | tf_op jit(solution)/shard_map/all_to_all | solution.py:163
  278.3 6.6 %copy.81 = f32[4096,375]{0,1:T(8,128)} copy(f32[4096,375]{1,0:T(8,128)} %bitcast.74) | data formatting | bytes 12288000
  288.2 130.0 %while.17 = (s32[]{:T(128)}, f32[125,4096]{1,0:T(8,128)}, f32[150,4096]{1,0:T(8,128)}, f32[4096,375]{0,1:T(8,128)}, s32[]{:T(128)}, /*index=5*/s32[]{:T(128)}, s...) while((s32[]{:T(128)}, f32[125,4096]{1,0:T(8,128)}, ...), condition=%wide.region_5.6_spmd.clone.clone, body=%wide.region_4.5_spmd.sunk.clone.clone.sunk | while | flops 866112000 | bytes 26822544 | solution.py:136
  424.2 4.9 copy.85
  429.1 21.0 %collective-permute-done.1 = f32[150,4096]{1,0:T(8,128)} collective-permute-done((f32[150,4096]{1,0:T(8,128)}, f32[150,4096]{1,0:T(8,128)}, u32[]{:S(2)}, u32[]{:S(2)}) %collective-permute-start.1) | collective-permute-done | bytes 2457632 | tf_op jit(solution)/shard_map/ppermute | solution.py:13
  450.1 4.8 copy.84
  454.9 3.3 copy.82
  458.2 11.9 %pad_maximum_fusion = f32[150,12288]{0,1:T(8,128)} fusion(f32[150,4096]{0,1:T(8,128)} %copy.84, f32[150,4096]{0,1:T(8,128)} %copy.85, f32[150,4096]{0,1:T(8,128)} %copy.82), kind=kLoop, calls=%fused_computation.32 | loop fusion | flops 3686400 | bytes 14745600 | tf_op jit(solution)/shard_map/concatenate | solution.py:177
  470.1 29.6 %fusion.14 = (f32[25,12288]{0,1:T(8,128)}, f32[25,12288]{0,1:T(8,128)}, f32[25,12288]{0,1:T(8,128)}, f32[25,12288]{0,1:T(8,128)}, f32[25,12288]{0,1:T(8,128)}, /*index=5*/f32[25,12288]{0,1:T(8,128)}) fusion(f32[150,12288]{0,1:T(8,128)} %pad_maximum_fusion), kind=kLoop, calls=%fused_computation.72 | loop fusion | bytes 14745600 | tf_op jit(solution)/shard_map/slice | solution.py:181
  499.7 17.0 %gather_fusion.2 = f32[4096,25]{1,0:T(8,128)} fusion(f32[25,12288]{0,1:T(8,128)} %get-tuple-element.292, s32[4096]{0:T(1024)S(1)} %fusion.9), kind=kCustom, calls=%fused_computation.1.clone | custom fusion | bytes 835584 | tf_op jit(solution)/shard_map/jit(_take)/gather | solution.py:181
  516.7 16.9 %gather_fusion.1 = f32[4096,25]{1,0:T(8,128)} fusion(f32[25,12288]{0,1:T(8,128)} %get-tuple-element.293, s32[4096]{0:T(1024)S(1)} %fusion.8), kind=kCustom, calls=%fused_computation.clone | custom fusion | bytes 835584 | tf_op jit(solution)/shard_map/jit(_take)/gather | solution.py:181
  533.6 16.9 %gather_fusion.4 = f32[4096,25]{1,0:T(8,128)} fusion(f32[25,12288]{0,1:T(8,128)} %get-tuple-element.290, s32[4096]{0:T(1024)S(1)} %fusion.11), kind=kCustom, calls=%fused_computation.3.clone | custom fusion | bytes 835584 | tf_op jit(solution)/shard_map/jit(_take)/gather | solution.py:181
  550.4 16.9 %gather_fusion.3 = f32[4096,25]{1,0:T(8,128)} fusion(f32[25,12288]{0,1:T(8,128)} %get-tuple-element.291, s32[4096]{0:T(1024)S(1)} %fusion.10), kind=kCustom, calls=%fused_computation.2.clone | custom fusion | bytes 835584 | tf_op jit(solution)/shard_map/jit(_take)/gather | solution.py:181
  567.3 16.9 %gather_fusion.6 = f32[4096,25]{1,0:T(8,128)} fusion(f32[25,12288]{0,1:T(8,128)} %get-tuple-element.288, s32[4096]{0:T(1024)S(1)} %fusion.13), kind=kCustom, calls=%fused_computation.5.clone | custom fusion | bytes 835584 | tf_op jit(solution)/shard_map/jit(_take)/gather | solution.py:181
  584.2 16.9 %gather_fusion.5 = f32[4096,25]{1,0:T(8,128)} fusion(f32[25,12288]{0,1:T(8,128)} %get-tuple-element.289, s32[4096]{0:T(1024)S(1)} %fusion.12), kind=kCustom, calls=%fused_computation.4.clone | custom fusion | bytes 835584 | tf_op jit(solution)/shard_map/jit(_take)/gather | solution.py:181
  601.1 6.4 %select_bitcast_fusion.4 = (f32[25,4096]{0,1:T(8,128)S(1)}, f32[25,4096]{0,1:T(8,128)}) fusion(f32[4096,25]{1,0:T(8,128)} %gather_fusion.2, pred[4096]{0:T(1024)(128)(4,1)S(1)} %compare_and_fusion.4, f32[4096,25]{1,0:T(8,128)} %gather_fusion.1, pred[4096]{0:T(1024)(128)(4,1)S(1)} %compare_and_fusion.5), kind=kLoop, calls=%fused_computation.39 | loop fusion | flops 204800 | bytes 1646592 | tf_op jit(solution)/shard_map/jit(_take)/select_n | solution.py:181
  607.6 4.4 select_bitcast_fusion.2
  612.0 4.4 select_bitcast_fusion
  616.4 9.2 %concatenate.14 = f32[150,4096]{0,1:T(8,128)} concatenate(f32[25,4096]{0,1:T(8,128)} %get-tuple-element.305, f32[25,4096]{0,1:T(8,128)S(1)} %get-tuple-element.304, f32[25,4096]{0,1:T(8,128)} %get-tuple-element.303, f32[25,4096]{0,1:T(8,128)} %get-tuple-element.302, f32[25,4096]{0,1:T(8,128)} %get-tuple-element.301, f32[25,4096]{0,1:T(8,128)} %get-tuple-element.300), dimensions={0} | concatenate | bytes 4915200 | tf_op jit(solution)/shard_map/concatenate | solution.py:182
  625.7 6.1 add.194
  631.7 5.0 copy.86
  (226 shorter events, 144.2 us)
Async XLA Ops:
  12.7 5.5 copy-start.10
  18.2 3.6 copy-start.6
  129.0 6.6 %copy-start.7 = (s32[4096,6]{0,1:T(8,128)S(1)}, s32[4096,6]{0,1:T(8,128)}, u32[]{:S(2)}) copy-start(s32[4096,6]{0,1:T(8,128)} %param.20) | copy-start | bytes 294916
  129.0 141.7 %all-to-all-start.1 = ((f32[4,8,128,375]{2,0,3,1:T(4,128)}), f32[4,8,128,375]{2,0,3,1:T(4,128)}, u32[]{:S(2)}, u32[]{:S(2)}) async-start(f32[4,8,128,375]{2,0,3,1:T(4,128)} %copy.79), calls=%async_computation.1 | async-start | bytes 12288000 | tf_op jit(solution)/shard_map/all_to_all | solution.py:163
  284.9 3.3 copy-start.1
  284.9 3.3 copy-start.8
  284.9 3.3 copy-start.9
  299.4 1.0 copy-start
  315.7 1.0 copy-start
  331.9 1.0 copy-start
  348.2 1.0 copy-start
  364.4 1.0 copy-start
  380.7 1.0 copy-start
  396.9 1.0 copy-start
  413.2 1.0 copy-start
  418.2 31.9 %collective-permute-start.1 = (f32[150,4096]{1,0:T(8,128)}, f32[150,4096]{1,0:T(8,128)}, u32[]{:S(2)}, u32[]{:S(2)}) collective-permute-start(f32[150,4096]{1,0:T(8,128)} %get-tuple-element.204), channel_id=1, source_target_pairs={{1,0},{2,1},{3,2},{4,3},{5,4},{6,5},{7,6},{9,8},{10,9},{11,10},{12... | collective-permute-start | bytes 7372808 | tf_op jit(solution)/shard_map/ppermute | solution.py:13
  421.0 33.9 %collective-permute-start = (f32[150,4096]{1,0:T(8,128)}, f32[150,4096]{1,0:T(8,128)S(1)}, u32[]{:S(2)}, u32[]{:S(2)}) collective-permute-start(f32[150,4096]{1,0:T(8,128)} %get-tuple-element.204), channel_id=1, source_target_pairs={{0,1},{1,2},{2,3},{3,4},{4,5},{5,6},{6,7},{8,9},{9,10},{10,11},{11... | collective-permute-start | bytes 7372808 | tf_op jit(solution)/shard_map/ppermute | solution.py:13
  601.1 6.4 %copy-start.3 = (f32[4096,25]{1,0:T(8,128)S(1)}, f32[4096,25]{1,0:T(8,128)}, u32[]{:S(2)}) copy-start(f32[4096,25]{1,0:T(8,128)} %gather_fusion.4) | copy-start | bytes 1228804
  601.1 6.4 %copy-start.4 = (f32[4096,25]{1,0:T(8,128)S(1)}, f32[4096,25]{1,0:T(8,128)}, u32[]{:S(2)}) copy-start(f32[4096,25]{1,0:T(8,128)} %gather_fusion.3) | copy-start | bytes 1228804
  607.5 4.5 copy-start.2
  607.5 4.5 copy-start.5
where the time goes:
time: 639 us; the launch traced here: 637 us
  local copies, waits for them, and re-layouts  285 us (45%)
  waiting for transfers between devices  156 us (24%)
  other arithmetic  89.8 us (14%)
  blocking collectives  72.9 us (11%)
  matrix products  19 us (3%)
  starting transfers between devices  12.4 us (2%)
    all_to_all x1, waiting for transfers between devices, body(): lax.all_to_all(lax.all_to_all(outgoing, 'seg', split_axis=0, concat_axis=...  135 us
    gather x6, local copies, waits for them, and re-layouts, body(): fetched.append(jnp.take(pool[opposite], face_link[:, face], axis=1))  101 us
    all_to_all x1, blocking collectives, body(): lax.all_to_all(outgoing, 'seg', split_axis=0, concat_axis=0, tiled=True)  72.9 us
    slice x2, local copies, waits for them, and re-layouts, body(): fetched.append(jnp.take(pool[opposite], face_link[:, face], axis=1))  29.7 us
    ppermute x2, waiting for transfers between devices, shifted(): return lax.ppermute(array, axis, pairs)  21 us
    add x8, other arithmetic, geometry(): jac[0][0] * (jac[1][1] * jac[2][2] - jac[1][2] * jac[2][1])  19.4 us
    squeeze x8, local copies, waits for them, and re-layouts, geometry(): deriv[:, first]  19.4 us
    sqrt x24, other arithmetic, geometry(): jnp.sqrt(normal_x * normal_x + normal_y * normal_y + normal_z * normal_z)  18.2 us
  transfers between devices with their start and end apart: 3, of which 2 were waited for; matrix products, arithmetic and copies ran while one was open for 2% of the time, Pallas kernels for 0%

commit v1 on v0

v1 whole, which is shorter than its diff:
```python
import math

import jax
import jax.numpy as jnp
import ml_dtypes
import numpy as np
from jax import lax
from jax.experimental import pallas as pl
from jax.experimental.pallas import tpu as pltpu
from jax.sharding import PartitionSpec as P


def shifted(array, axis, by):
    count = lax.axis_size(axis)
    pairs = [(i, i + by) for i in range(count) if 0 <= i + by < count]
    return lax.ppermute(array, axis, pairs)


def gll_tables():
    points = np.array([-1.0, -math.sqrt(3.0 / 7.0), 0.0, math.sqrt(3.0 / 7.0), 1.0])
    weights = np.array([0.1, 49.0 / 90.0, 32.0 / 45.0, 49.0 / 90.0, 0.1])
    barycentric = np.array(
        [1.0 / np.prod([points[j] - points[m] for m in range(5) if m != j]) for j in range(5)]
    )
    slopes = np.zeros((5, 5))
    for i in range(5):
        for j in range(5):
            if i != j:
                slopes[i, j] = barycentric[j] / barycentric[i] / (points[i] - points[j])
        slopes[i, i] = -np.sum(slopes[i])

    def lagrange_at(where):
        table = np.ones((5, 5))
        for a in range(5):
            for j in range(5):
                for m in range(5):
                    if m != j:
                        table[a, j] *= (where[a] - points[m]) / (points[j] - points[m])
        return table

    def blend(value, side):
        return (1.0 - value) / 2.0 if side == 0 else (1.0 + value) / 2.0

    def flat(i, j, k):
        return i * 25 + j * 5 + k

    ends = (0, 4)
    gordon = np.zeros((125, 125))
    for i in range(5):
        for j in range(5):
            for k in range(5):
                r, s, t = (points[i], points[j], points[k])
                target = flat(i, j, k)
                for a in range(2):
                    gordon[target, flat(ends[a], j, k)] += blend(r, a)
                    gordon[target, flat(i, ends[a], k)] += blend(s, a)
                    gordon[target, flat(i, j, ends[a])] += blend(t, a)
                    for b in range(2):
                        gordon[target, flat(ends[a], ends[b], k)] -= blend(r, a) * blend(s, b)
                        gordon[target, flat(ends[a], j, ends[b])] -= blend(r, a) * blend(t, b)
                        gordon[target, flat(i, ends[a], ends[b])] -= blend(s, a) * blend(t, b)
                        for c in range(2):
                            gordon[target, flat(ends[a], ends[b], ends[c])] += (
                                blend(r, a) * blend(s, b) * blend(t, c)
                            )
    identity = np.eye(5)
    derivs = [
        np.kron(np.kron(slopes, identity), identity),
        np.kron(np.kron(identity, slopes), identity),
        np.kron(np.kron(identity, identity), slopes),
    ]
    mass_weights = np.kron(np.kron(weights, weights), weights)
    face_weights = np.kron(weights, weights)
    tangents = [(1, 2), (1, 2), (0, 2), (0, 2), (0, 1), (0, 1)]
    boundary = [
        flat(i, j, k)
        for i in range(5)
        for j in range(5)
        for k in range(5)
        if i in ends or j in ends or k in ends
    ]
    halves = [lagrange_at((points - 1.0) / 2.0), lagrange_at((points + 1.0) / 2.0)]
    steps = [
        [np.kron(np.kron(half, identity), identity) @ gordon for half in halves],
        [np.kron(np.kron(identity, half), identity) for half in halves],
        [np.kron(np.kron(identity, identity), half) for half in halves],
    ]
    nodes = []
    for side in (0, 4):
        nodes.append([flat(side, j, k) for j in range(5) for k in range(5)])
    for side in (0, 4):
        nodes.append([flat(i, side, k) for i in range(5) for k in range(5)])
    for side in (0, 4):
        nodes.append([flat(i, j, side) for i in range(5) for j in range(5)])
    corners = [flat(i, j, k) for i in ends for j in ends for k in ends]
    return (steps, derivs, mass_weights, face_weights, nodes, tangents, boundary, corners)


HELD = 104
OWNERS = 3 * HELD
WIDTH = 256
NT = (((1,), (1,)), ((), ()))


def parts_of(table):
    high = table.astype(ml_dtypes.bfloat16)
    low = (table - high.astype(np.float64)).astype(ml_dtypes.bfloat16)
    return jnp.asarray(np.concatenate([high, high, low], axis=1))


def padded(table, rows, columns):
    out = np.zeros((rows, columns))
    out[: table.shape[0], : table.shape[1]] = table
    return out


def operators():
    steps, derivs, mass_weights, face_weights, nodes, tangents, boundary, corners = gll_tables()
    pick = np.zeros((OWNERS, 375))
    for c in range(3):
        for row, node in enumerate(boundary):
            pick[c * HELD + row, c * 125 + node] += 1.0
            for corner in corners:
                pick[c * HELD + row, c * 125 + corner] -= 0.125
    first = np.concatenate([padded(step[:, boundary], 128, HELD) for step in steps[0]])
    second = np.concatenate([padded(step, 128, 128) for step in steps[1]])
    third = np.concatenate([padded(step, 128, 128) for step in steps[2]])
    rows = [padded(derivs[0] * mass_weights[:, None], 128, 128)]
    rows += [padded(derivs[d], 128, 128) for d in (1, 2)]
    along = [derivs[tangents[f][0]][nodes[f]] * face_weights[:, None] for f in range(6)]
    across = [derivs[tangents[f][1]][nodes[f]] for f in range(6)]
    rows += [padded(np.concatenate(part), 152, 128) for part in (along, across)]
    return pick, [parts_of(table) for table in (first, second, third, np.concatenate(rows))]


def stacked(values):
    high = values.astype(jnp.bfloat16)
    low = (values - high.astype(jnp.float32)).astype(jnp.bfloat16)
    return jnp.concatenate([high, low, high], axis=0)


def geometry_kernel(cap, block_ref, mask_ref, a1_ref, a2_ref, a3_ref, ad_ref, mass_ref, face_ref, place_ref):
    step = pl.program_id(0)
    group = WIDTH // cap
    f32 = jnp.float32

    @pl.when(step == 0)
    def _():
        row = lax.broadcasted_iota(jnp.int32, (256, 256), 0)
        column = lax.broadcasted_iota(jnp.int32, (256, 256), 1)
        earlier = (row < column).astype(f32).astype(jnp.bfloat16)
        same = (row // 8 == column // 8).astype(f32).astype(jnp.bfloat16)
        within = ((row // 8 == column // 8) & (column < row)).astype(f32).astype(jnp.bfloat16)
        for chunk in range(mask_ref.shape[0] // 256):
            mask = mask_ref[chunk * 256 : (chunk + 1) * 256, :]
            small = mask.astype(jnp.bfloat16)
            before = jnp.dot(small, earlier, preferred_element_type=f32).astype(jnp.bfloat16)
            count = jnp.dot(same, before, preferred_element_type=f32)
            count += jnp.dot(within, small, preferred_element_type=f32)
            place_ref[chunk * 256 : (chunk + 1) * 256, :] = jnp.where(mask > 0.5, count, -1e6)

    span = cap if cap % 128 == 0 else WIDTH
    slot = lax.broadcasted_iota(jnp.int32, (span, 256), 0).astype(f32)
    gathered, octants = [], []
    for s in range(group):
        places = place_ref[pl.ds(pl.multiple_of((step * group + s) * 8, 8), 8), :]
        if span != cap:
            places = places + float(s * cap)
        hit = jnp.zeros((span, 256), f32)
        for o in range(8):
            hit = jnp.where(places[o : o + 1, :] == slot, float(o + 1), hit)
        block = block_ref[s, :OWNERS, :]
        high = block.astype(jnp.bfloat16).astype(f32)
        both = jnp.concatenate([high, block - high], axis=0).astype(jnp.bfloat16)
        chosen = jnp.where(hit > 0.5, 1.0, 0.0).astype(jnp.bfloat16)
        gathered.append(lax.dot_general(both, chosen, NT, preferred_element_type=f32))
        octants.append(
            lax.dot_general(
                jnp.ones((8, 256), jnp.bfloat16), hit.astype(jnp.bfloat16), NT, preferred_element_type=f32
            )
        )
    if span == cap:
        held = jnp.concatenate(gathered, axis=1)
        octant = jnp.concatenate(octants, axis=1)
    else:
        held = sum(gathered[1:], gathered[0])
        octant = sum(octants[1:], octants[0])
    octant = octant[0:1, :]
    bits = []
    for size in (4.0, 2.0, 1.0):
        bit = jnp.where(octant > size + 0.5, 1.0, 0.0)
        octant = octant - size * bit
        bits.append(jnp.concatenate([bit, bit, bit], axis=1))
    high = jnp.concatenate([held[c * HELD : (c + 1) * HELD] for c in range(3)], axis=1)
    low = jnp.concatenate([held[(c + 3) * HELD : (c + 4) * HELD] for c in range(3)], axis=1)
    operand = jnp.concatenate([high, low, high], axis=0).astype(jnp.bfloat16)
    for table_ref, bit in zip((a1_ref, a2_ref, a3_ref), bits):
        sides = jnp.dot(table_ref[...], operand, preferred_element_type=f32)
        operand = stacked(jnp.where(bit > 0.5, sides[128:], sides[:128]))

    def components(start, rows):
        table = ad_ref[start : start + rows, :]
        values = jnp.dot(table, operand, preferred_element_type=f32)
        return [values[:, c * WIDTH : (c + 1) * WIDTH] for c in range(3)]

    def crossed(p, q):
        return [p[1] * q[2] - p[2] * q[1], p[2] * q[0] - p[0] * q[2], p[0] * q[1] - p[1] * q[0]]

    first, second, third = (components(128 * d, 128) for d in range(3))
    normal = crossed(second, third)
    mass_ref[...] = (first[0] * normal[0] + first[1] * normal[1] + first[2] * normal[2])[:125]
    normal = crossed(components(384, 152), components(536, 152))
    face_ref[...] = jnp.sqrt(normal[0] * normal[0] + normal[1] * normal[1] + normal[2] * normal[2])


def whole_spec(array):
    return pl.BlockSpec(array.shape, lambda i: (0,) * array.ndim)


def geometry(blocks, mask, tables, cap):
    devices = blocks.shape[0]
    slots = devices * cap
    group = WIDTH // cap
    return pl.pallas_call(
        lambda *refs: geometry_kernel(cap, *refs),
        grid=(slots // WIDTH,),
        in_specs=[pl.BlockSpec((group,) + blocks.shape[1:], lambda i: (i, 0, 0)), whole_spec(mask)]
        + [whole_spec(table) for table in tables],
        out_specs=[
            pl.BlockSpec((125, WIDTH), lambda i: (0, i)),
            pl.BlockSpec((152, WIDTH), lambda i: (0, i)),
        ],
        out_shape=[
            jax.ShapeDtypeStruct((125, slots), jnp.float32),
            jax.ShapeDtypeStruct((152, slots), jnp.float32),
        ],
        scratch_shapes=[pltpu.VMEM(mask.shape, jnp.float32)],
        compiler_params=pltpu.CompilerParams(vmem_limit_bytes=48 * 1024 * 1024),
        name="geometry",
    )(blocks, mask, *tables)


def assemble_kernel(link_ref, before_ref, own_ref, after_ref, out_ref, low_ref, high_ref, row_low, row_high):
    slots = own_ref.shape[1]
    for part, ref in enumerate((before_ref, own_ref, after_ref)):

        @pl.loop(0, slots // 128)
        def _(number):
            start = pl.multiple_of(number * 128, 128)
            rows = pl.ds(pl.multiple_of(part * slots + number * 128, 128), 128)
            low_ref[rows, :] = ref[0:128, pl.ds(start, 128)].T
            high_ref[rows, :] = ref[24:152, pl.ds(start, 128)].T

    lane = lax.broadcasted_iota(jnp.int32, (1, 128), 1)
    under = [lane < 25 * (g + 1) for g in range(4)]

    @pl.loop(0, slots // 128)
    def _(number):
        start = pl.multiple_of(number * 128, 128)

        @pl.loop(0, 128, step=16)
        def _(inner):
            for k in range(16):
                u = start + inner + k
                row = [link_ref[f * slots + u] for f in range(6)]
                value = low_ref[pl.ds(row[5], 1), :]
                for g in (3, 2, 1, 0):
                    value = jnp.where(under[g], low_ref[pl.ds(row[g ^ 1], 1), :], value)
                row_low[pl.ds(inner + k, 1), :] = value
                row_high[pl.ds(inner + k, 1), :] = high_ref[pl.ds(row[4], 1), :]

        low = row_low[...].T
        high = row_high[...].T
        fetched = [low[25 * (f ^ 1) : 25 * (f ^ 1) + 25] for f in range(4)]
        fetched += [high[101:126], low[100:125]]
        total = own_ref[0:150, pl.ds(start, 128)] + jnp.concatenate(fetched, axis=0)
        out_ref[:, pl.ds(start, 128)] = total


def assemble(link, before, own, after):
    slots = own.shape[1]
    vmem = pl.BlockSpec(memory_space=pltpu.VMEM)
    return pl.pallas_call(
        assemble_kernel,
        in_specs=[pl.BlockSpec(memory_space=pltpu.SMEM), vmem, vmem, vmem],
        out_specs=vmem,
        out_shape=jax.ShapeDtypeStruct((150, slots), jnp.float32),
        scratch_shapes=[
            pltpu.VMEM((3 * slots, 128), jnp.float32),
            pltpu.VMEM((3 * slots, 128), jnp.float32),
            pltpu.VMEM((128, 128), jnp.float32),
            pltpu.VMEM((128, 128), jnp.float32),
        ],
        compiler_params=pltpu.CompilerParams(vmem_limit_bytes=48 * 1024 * 1024),
        name="assemble",
    )(link, before, own, after)


def body(parent_nodes, marks, child_owner, face_link):
    pick, tables = operators()
    devices = lax.axis_size("seg") * lax.axis_size("rank")
    me = lax.axis_index("seg") * lax.axis_size("rank") + lax.axis_index("rank")
    kids = child_owner.shape[0]
    cap = max(2, 2 * kids // devices)
    picked = parent_nodes[marks[0]]
    coords = lax.dot_general(
        jnp.asarray(pick, jnp.float32),
        picked,
        NT,
        precision=lax.Precision.HIGHEST,
        preferred_element_type=jnp.float32,
    )
    owners = child_owner.reshape(kids // 8, 8).T.astype(jnp.float32)
    block = jnp.concatenate([coords, owners], axis=0)
    blocks = lax.all_gather(block, ("seg", "rank"))
    mask = (blocks[:, OWNERS:, :] == me.astype(jnp.float32)).astype(jnp.float32)
    mass, faces = geometry(blocks, mask.reshape(devices * 8, kids // 8), tables, cap)
    before = shifted(faces, "rank", 1)
    after = shifted(faces, "rank", -1)
    return (mass, assemble(face_link.T.reshape(-1), before, faces, after))


def solution(mesh):
    return jax.shard_map(
        body,
        mesh=mesh,
        in_specs=(
            P(("seg", "rank"), None),
            P(("seg", "rank"), None),
            P(("seg", "rank"), None),
            P(("seg", "rank"), None),
        ),
        out_specs=(P(None, ("seg", "rank")), P(None, ("seg", "rank"))),
        check_vma=False,
    )
```

time: 639 us -> 225 us (0.35)
  local copies, waits for them, and re-layouts: 285 us -> 10 us
  other arithmetic: 89.8 us -> 1.75 us
  Pallas kernels: 0 us -> 73.6 us
  blocking collectives: 72.9 us -> 0 us
  waiting for transfers between devices: 156 us -> 118 us
  matrix products: 19 us -> 0.68 us
  between operations: 0.85 us -> 14.2 us
  starting transfers between devices: 12.4 us -> 5.8 us
    all_to_all x1 -> x0, waiting for transfers between devices: 135 us -> none  [body(): lax.all_to_all(lax.all_to_all(outgoing, 'seg', split_axis=0, concat_axis=...]
    gather x6 -> x0, local copies, waits for them, and re-layouts: 101 us -> none  [body(): fetched.append(jnp.take(pool[opposite], face_link[:, face], axis=1))]
    all_gather x0 -> x1, waiting for transfers between devices: none -> 89.5 us  [body(): blocks = lax.all_gather(block, ('seg', 'rank'))]
    pallas_call x0 -> x2, Pallas kernels: none -> 73.6 us  [the longest x1 37.7 us: assemble(): pl.pallas_call(assemble_kernel, in_specs=[pl.BlockSpec(memory_space=pltpu...]
    all_to_all x1 -> x0, blocking collectives: 72.9 us -> none  [body(): lax.all_to_all(outgoing, 'seg', split_axis=0, concat_axis=0, tiled=True)]
    slice x2 -> x0, local copies, waits for them, and re-layouts: 29.7 us -> none  [body(): fetched.append(jnp.take(pool[opposite], face_link[:, face], axis=1))]
    reshape x18 -> x1, local copies, waits for them, and re-layouts: 29.2 us -> 0.05 us  [body(): return (mass, assemble(face_link.T.reshape(-1), before, faces, after))]
    add x9 -> x0, other arithmetic: 25.5 us -> none  [the longest x8 19.4 us: geometry(): jac[0][0] * (jac[1][1] * jac[2][2] - jac[1][2] * jac[2][1])]
  transfers between devices with their start and end apart: 3 -> 3, of which waited for: 2 -> 3; matrix products, arithmetic and copies ran while one was open for 2% -> 0% of each run, Pallas kernels for 0% -> 0%
where the time goes in v1:
time: 225 us; the launch traced here: 224 us
  waiting for transfers between devices  118 us (52%)
  Pallas kernels  73.6 us (33%)
  between operations  14.2 us (6%)
  local copies, waits for them, and re-layouts  10 us (4%)
  starting transfers between devices  5.8 us (3%)
    all_gather x1, waiting for transfers between devices, body(): blocks = lax.all_gather(block, ('seg', 'rank'))  89.5 us
    pallas_call x1, Pallas kernels, assemble(): pl.pallas_call(assemble_kernel, in_specs=[pl.BlockSpec(memory_space=pltpu...  37.7 us
    pallas_call x1, Pallas kernels, geometry(): pl.pallas_call(lambda *refs: geometry_kernel(cap, *refs), grid=(slots //...  35.9 us
    ppermute x2, waiting for transfers between devices, shifted(): return lax.ppermute(array, axis, pairs)  28.9 us
    unnamed x17, local copies, waits for them, and re-layouts  6.45 us
    ppermute x2, starting transfers between devices, shifted(): return lax.ppermute(array, axis, pairs)  5.76 us
  transfers between devices with their start and end apart: 3, of which 3 were waited for; matrix products, arithmetic and copies ran while one was open for 0% of the time, Pallas kernels for 0%

profile of v1, /device:TPU:1, one launch (start us, length us, event | category | flops | bytes accessed | tf_op | source)
XLA Modules:
  0.0 224.4 jit_solution(6926234508591074723)
XLA Ops:
  7.2 0.0 copy-start.7
  7.2 0.0 copy-start.6
  7.2 0.0 all-gather.3.cloned.1.call-start
  7.2 5.5 %copy.12 = f32[2560,375]{1,0:T(8,128)} copy(f32[2560,375]{0,1:T(8,128)} %param.9) | data formatting | bytes 7680000 | tf_op args[0]
  12.7 0.0 copy-done.7
  12.7 0.0 copy-start.4
  12.7 0.0 copy-start
  12.7 0.0 copy-start.1
  12.7 0.0 copy-start.2
  12.8 0.0 copy-done.6
  12.8 0.1 convert_element_type.14
  12.9 0.1 copy.13
  13.0 3.4 %gather_fusion = f32[256,375]{1,0:T(8,128)S(1)} fusion(f32[2560,375]{1,0:T(8,128)} %copy.12, s32[1024]{0:T(1024)S(1)} %pad_clamp_fusion), kind=kCustom, calls=%fused_computation | custom fusion | bytes 769024 | tf_op jit(solution)/shard_map/gather | solution.py:305
  16.4 0.0 copy-done.4
  16.4 0.7 fusion
  17.1 0.7 pad_maximum_fusion
  17.8 0.0 all-gather.3.cloned.1.call-update
  17.9 89.5 %all-gather.3.cloned.1.call-done = f32[10240,256]{1,0:T(8,128)} async-done(((f32[320,256]{1,0:T(8,128)}), f32[10240,256]{1,0:T(8,128)}) %all-gather.3.cloned.1.call-update) | async-done | bytes 10485776 | tf_op jit(solution)/shard_map/all_gather | solution.py:315
  107.3 1.0 convert_bitcast_fusion.refs_1_
  108.3 0.0 copy-done
  108.3 0.0 copy-done.1
  108.3 0.0 copy-done.2
  108.3 0.0 copy-start.3
  108.4 0.9 copy-done.3
  109.3 35.9 %geometry.1 = (f32[125,4096]{1,0:T(8,128)}, f32[152,4096]{1,0:T(8,128)S(1)}) custom-call(f32[32,320,256]{2,1,0:T(8,128)} %bitcast.11, f32[256,256]{1,0:T(8,128)S(1)} %convert_bitcast_fusion.refs_1_, bf16[256,312]{1,0:T(8,128)(2,1)S(1)} %copy-done.1, bf16[256,384]{1,0:T(8,128)(2,1)S(1)} %copy-done.2, bf16[256,384]{1,0:T(8,128)(2,1)S(1)} %copy-done.3, ...), custom_call_target="tpu_custom_call" | custom-call | tf_op jit(solution)/shard_map/geometry/pallas_call | solution.py:224
  145.1 3.1 %collective-permute-start = (f32[152,4096]{1,0:T(8,128)S(1)}, f32[152,4096]{1,0:T(8,128)}, u32[]{:S(2)}, u32[]{:S(2)}) collective-permute-start(f32[152,4096]{1,0:T(8,128)S(1)} %get-tuple-element.5.own_ref), channel_id=1, source_target_pairs={{0,1},{1,2},{2,3},{3,4},{4,5},{5,6},{6,7},{8,9},{9,10},{10,11},{11... | collective-permute-start | bytes 7471112 | tf_op jit(solution)/shard_map/ppermute | solution.py:16
  148.2 2.7 %collective-permute-start.1 = (f32[152,4096]{1,0:T(8,128)S(1)}, f32[152,4096]{1,0:T(8,128)}, u32[]{:S(2)}, u32[]{:S(2)}) collective-permute-start(f32[152,4096]{1,0:T(8,128)S(1)} %get-tuple-element.5.own_ref), channel_id=1, source_target_pairs={{1,0},{2,1},{3,2},{4,3},{5,4},{6,5},{7,6},{9,8},{10,9},{11,10},{12... | collective-permute-start | bytes 7471112 | tf_op jit(solution)/shard_map/ppermute | solution.py:16
  150.9 0.0 copy-done.5
  150.9 0.1 reshape.44.link_ref
  151.0 24.4 %collective-permute-done.before_ref = f32[152,4096]{1,0:T(8,128)} collective-permute-done((f32[152,4096]{1,0:T(8,128)S(1)}, f32[152,4096]{1,0:T(8,128)}, u32[]{:S(2)}, u32[]{:S(2)}) %collective-permute-start) | collective-permute-done | bytes 2490400 | tf_op jit(solution)/shard_map/ppermute | solution.py:16
  175.4 4.5 %collective-permute-done.1.after_ref = f32[152,4096]{1,0:T(8,128)} collective-permute-done((f32[152,4096]{1,0:T(8,128)S(1)}, f32[152,4096]{1,0:T(8,128)}, u32[]{:S(2)}, u32[]{:S(2)}) %collective-permute-start.1) | collective-permute-done | bytes 2490400 | tf_op jit(solution)/shard_map/ppermute | solution.py:16
  179.9 37.7 %assemble.1 = f32[150,4096]{1,0:T(8,128)} custom-call(s32[24576]{0:T(1024)S(1)} %reshape.44.link_ref, f32[152,4096]{1,0:T(8,128)} %collective-permute-done.before_ref, f32[152,4096]{1,0:T(8,128)S(1)} %get-tuple-element.5.own_ref, f32[152,4096]{1,0:T(8,128)} %collective-permute-done.1.after_ref), custom_call_target="tpu_custom_call" | custom-call | tf_op jit(solution)/shard_map/assemble/pallas_call | solution.py:283
  (4 shorter events, 0.0 us)
Async XLA Ops:
  7.2 5.6 %copy-start.7 = (s32[1,256]{1,0:T(1,128)S(1)}, s32[1,256]{1,0:T(1,128)}, u32[]{:S(2)}) copy-start(s32[1,256]{1,0:T(1,128)} %param.10) | copy-start | bytes 3076
  7.2 5.6 %copy-start.6 = (s32[2048,1]{0,1:T(1,128)S(1)}, s32[2048,1]{0,1:T(1,128)}, u32[]{:S(2)}) copy-start(s32[2048,1]{0,1:T(1,128)} %param.11) | copy-start | bytes 24580
  7.2 100.2 %all-gather.3.cloned.1.call-start = ((), (), s32[]{:S(2)}) async-start(), calls=%async_computation | async-start | bytes 10813440 | tf_op jit(solution)/shard_map/all_gather | solution.py:315
  12.7 3.7 %copy-start.4 = (f32[312,375]{1,0:T(8,128)S(1)}, f32[312,375]{1,0:T(8,128)}, u32[]{:S(2)}) copy-start(f32[312,375]{1,0:T(8,128)} %constant.28.clone) | copy-start | bytes 1404004
  12.7 95.6 %copy-start = (bf16[688,384]{1,0:T(8,128)(2,1)S(1)}, bf16[688,384]{1,0:T(8,128)(2,1)}, u32[]{:S(2)}) copy-start(bf16[688,384]{1,0:T(8,128)(2,1)} %constant.27.clone.refs_5_) | copy-start | bytes 1585156
  12.7 95.6 %copy-start.1 = (bf16[256,312]{1,0:T(8,128)(2,1)S(1)}, bf16[256,312]{1,0:T(8,128)(2,1)}, u32[]{:S(2)}) copy-start(bf16[256,312]{1,0:T(8,128)(2,1)} %constant.24.clone.refs_2_) | copy-start | bytes 479236
  12.7 95.6 %copy-start.2 = (bf16[256,384]{1,0:T(8,128)(2,1)S(1)}, bf16[256,384]{1,0:T(8,128)(2,1)}, u32[]{:S(2)}) copy-start(bf16[256,384]{1,0:T(8,128)(2,1)} %constant.25.clone.refs_3_) | copy-start | bytes 589828
  108.3 0.9 copy-start.3
  109.3 41.7 %copy-start.5 = (s32[4096,6]{0,1:T(8,128)S(1)}, s32[4096,6]{0,1:T(8,128)}, u32[]{:S(2)}) copy-start(s32[4096,6]{0,1:T(8,128)} %param.12) | copy-start | bytes 294916
  145.1 30.3 %collective-permute-start = (f32[152,4096]{1,0:T(8,128)S(1)}, f32[152,4096]{1,0:T(8,128)}, u32[]{:S(2)}, u32[]{:S(2)}) collective-permute-start(f32[152,4096]{1,0:T(8,128)S(1)} %get-tuple-element.5.own_ref), channel_id=1, source_target_pairs={{0,1},{1,2},{2,3},{3,4},{4,5},{5,6},{6,7},{8,9},{9,10},{10,11},{11... | collective-permute-start | bytes 7471112 | tf_op jit(solution)/shard_map/ppermute | solution.py:16
  148.2 31.7 %collective-permute-start.1 = (f32[152,4096]{1,0:T(8,128)S(1)}, f32[152,4096]{1,0:T(8,128)}, u32[]{:S(2)}, u32[]{:S(2)}) collective-permute-start(f32[152,4096]{1,0:T(8,128)S(1)} %get-tuple-element.5.own_ref), channel_id=1, source_target_pairs={{1,0},{2,1},{3,2},{4,3},{5,4},{6,5},{7,6},{9,8},{10,9},{11,10},{12... | collective-permute-start | bytes 7471112 | tf_op jit(solution)/shard_map/ppermute | solution.py:16
Sparse Core Ops, SparseCore 0:
  18.0 89.3 all-gather.2

commit v2 on v1

--- a/solution.py
+++ b/solution.py
@@ -1,3 +1,4 @@
+import functools
 import math
 
 import jax
@@ -130,7 +131,8 @@
     along = [derivs[tangents[f][0]][nodes[f]] * face_weights[:, None] for f in range(6)]
     across = [derivs[tangents[f][1]][nodes[f]] for f in range(6)]
     rows += [padded(np.concatenate(part), 152, 128) for part in (along, across)]
-    return pick, [parts_of(table) for table in (first, second, third, np.concatenate(rows))]
+    earlier = jnp.asarray(np.triu(np.ones((256, 256)), 1).astype(ml_dtypes.bfloat16))
+    return pick, [earlier] + [parts_of(table) for table in (first, second, third, np.concatenate(rows))]
 
 
 def stacked(values):
@@ -139,58 +141,34 @@
     return jnp.concatenate([high, low, high], axis=0)
 
 
-def geometry_kernel(cap, block_ref, mask_ref, a1_ref, a2_ref, a3_ref, ad_ref, mass_ref, face_ref, place_ref):
-    step = pl.program_id(0)
-    group = WIDTH // cap
-    f32 = jnp.float32
-
-    @pl.when(step == 0)
-    def _():
-        row = lax.broadcasted_iota(jnp.int32, (256, 256), 0)
-        column = lax.broadcasted_iota(jnp.int32, (256, 256), 1)
-        earlier = (row < column).astype(f32).astype(jnp.bfloat16)
-        same = (row // 8 == column // 8).astype(f32).astype(jnp.bfloat16)
-        within = ((row // 8 == column // 8) & (column < row)).astype(f32).astype(jnp.bfloat16)
-        for chunk in range(mask_ref.shape[0] // 256):
-            mask = mask_ref[chunk * 256 : (chunk + 1) * 256, :]
-            small = mask.astype(jnp.bfloat16)
-            before = jnp.dot(small, earlier, preferred_element_type=f32).astype(jnp.bfloat16)
-            count = jnp.dot(same, before, preferred_element_type=f32)
-            count += jnp.dot(within, small, preferred_element_type=f32)
-            place_ref[chunk * 256 : (chunk + 1) * 256, :] = jnp.where(mask > 0.5, count, -1e6)
-
-    span = cap if cap % 128 == 0 else WIDTH
-    slot = lax.broadcasted_iota(jnp.int32, (span, 256), 0).astype(f32)
-    gathered, octants = [], []
-    for s in range(group):
-        places = place_ref[pl.ds(pl.multiple_of((step * group + s) * 8, 8), 8), :]
-        if span != cap:
-            places = places + float(s * cap)
-        hit = jnp.zeros((span, 256), f32)
-        for o in range(8):
-            hit = jnp.where(places[o : o + 1, :] == slot, float(o + 1), hit)
-        block = block_ref[s, :OWNERS, :]
-        high = block.astype(jnp.bfloat16).astype(f32)
-        both = jnp.concatenate([high, block - high], axis=0).astype(jnp.bfloat16)
-        chosen = jnp.where(hit > 0.5, 1.0, 0.0).astype(jnp.bfloat16)
-        gathered.append(lax.dot_general(both, chosen, NT, preferred_element_type=f32))
-        octants.append(
-            lax.dot_general(
-                jnp.ones((8, 256), jnp.bfloat16), hit.astype(jnp.bfloat16), NT, preferred_element_type=f32
-            )
-        )
-    if span == cap:
-        held = jnp.concatenate(gathered, axis=1)
-        octant = jnp.concatenate(octants, axis=1)
-    else:
-        held = sum(gathered[1:], gathered[0])
-        octant = sum(octants[1:], octants[0])
-    octant = octant[0:1, :]
+def octant_bits(octant):
     bits = []
     for size in (4.0, 2.0, 1.0):
         bit = jnp.where(octant > size + 0.5, 1.0, 0.0)
         octant = octant - size * bit
         bits.append(jnp.concatenate([bit, bit, bit], axis=1))
+    return bits
+
+
+def chosen_children(block, keys, span):
+    f32 = jnp.float32
+    slot = lax.broadcasted_iota(jnp.int32, (span, 256), 0).astype(f32)
+    hit = jnp.zeros((span, 256), f32)
+    for o in range(8):
+        hit = jnp.where(keys[o] == slot, float(o + 1), hit)
+    high = block.astype(jnp.bfloat16).astype(f32)
+    both = jnp.concatenate([high, block - high], axis=0).astype(jnp.bfloat16)
+    chosen = jnp.where(hit > 0.5, 1.0, 0.0).astype(jnp.bfloat16)
+    held = lax.dot_general(both, chosen, NT, preferred_element_type=f32)
+    octant = lax.dot_general(
+        jnp.ones((8, 256), jnp.bfloat16), hit.astype(jnp.bfloat16), NT, preferred_element_type=f32
+    )
+    return held, octant
+
+
+def masses(held, octant, a1_ref, a2_ref, a3_ref, ad_ref):
+    f32 = jnp.float32
+    bits = octant_bits(octant[0:1, :])
     high = jnp.concatenate([held[c * HELD : (c + 1) * HELD] for c in range(3)], axis=1)
     low = jnp.concatenate([held[(c + 3) * HELD : (c + 4) * HELD] for c in range(3)], axis=1)
     operand = jnp.concatenate([high, low, high], axis=0).astype(jnp.bfloat16)
@@ -208,9 +186,42 @@
 
     first, second, third = (components(128 * d, 128) for d in range(3))
     normal = crossed(second, third)
-    mass_ref[...] = (first[0] * normal[0] + first[1] * normal[1] + first[2] * normal[2])[:125]
+    mass = (first[0] * normal[0] + first[1] * normal[1] + first[2] * normal[2])[:125]
     normal = crossed(components(384, 152), components(536, 152))
-    face_ref[...] = jnp.sqrt(normal[0] * normal[0] + normal[1] * normal[1] + normal[2] * normal[2])
+    face = jnp.sqrt(normal[0] * normal[0] + normal[1] * normal[1] + normal[2] * normal[2])
+    return mass, face
+
+
+def keys_of(mask, earlier):
+    before = jnp.dot(mask.astype(jnp.bfloat16), earlier, preferred_element_type=jnp.float32)
+    total = jnp.sum(before, axis=0, keepdims=True)
+    keys = []
+    for o in range(8):
+        row = mask[o : o + 1, :]
+        keys.append(jnp.where(row > 0.5, total, -1e6))
+        total = total + row
+    return keys
+
+
+def geometry_kernel(cap, block_ref, mask_ref, earlier_ref, a1_ref, a2_ref, a3_ref, ad_ref, mass_ref, face_ref):
+    gathered, octants = [], []
+    aligned = cap % 128 == 0
+    for s in range(WIDTH // cap):
+        keys = keys_of(mask_ref[s], earlier_ref[...])
+        if not aligned:
+            keys = [key + float(s * cap) for key in keys]
+        held, octant = chosen_children(block_ref[s, :OWNERS, :], keys, cap if aligned else WIDTH)
+        gathered.append(held)
+        octants.append(octant)
+    if aligned:
+        held = jnp.concatenate(gathered, axis=1)
+        octant = jnp.concatenate(octants, axis=1)
+    else:
+        held = sum(gathered[1:], gathered[0])
+        octant = sum(octants[1:], octants[0])
+    mass, face = masses(held, octant, a1_ref, a2_ref, a3_ref, ad_ref)
+    mass_ref[...] = mass
+    face_ref[...] = face
 
 
 def whole_spec(array):
@@ -224,7 +235,10 @@
     return pl.pallas_call(
         lambda *refs: geometry_kernel(cap, *refs),
         grid=(slots // WIDTH,),
-        in_specs=[pl.BlockSpec((group,) + blocks.shape[1:], lambda i: (i, 0, 0)), whole_spec(mask)]
+        in_specs=[
+            pl.BlockSpec((group,) + blocks.shape[1:], lambda i: (i, 0, 0)),
+            pl.BlockSpec((group,) + mask.shape[1:], lambda i: (i, 0, 0)),
+        ]
         + [whole_spec(table) for table in tables],
         out_specs=[
             pl.BlockSpec((125, WIDTH), lambda i: (0, i)),
@@ -234,10 +248,242 @@
             jax.ShapeDtypeStruct((125, slots), jnp.float32),
             jax.ShapeDtypeStruct((152, slots), jnp.float32),
         ],
-        scratch_shapes=[pltpu.VMEM(mask.shape, jnp.float32)],
         compiler_params=pltpu.CompilerParams(vmem_limit_bytes=48 * 1024 * 1024),
         name="geometry",
     )(blocks, mask, *tables)
+
+
+MESH = pl.DeviceIdType.MESH
+CHIP_Z = 4
+
+
+def gather_kernel(
+    block_ref, earlier_ref, a1_ref, a2_ref, a3_ref, ad_ref,
+    mass_ref, face_ref, before_ref, after_ref, held_ref,
+    send_up, send_down, send_x, send_y, send_dx, send_dy, send_c, send_next, send_prev,
+    recv_z, recv_x, recv_y, recv_dx, recv_dy, recv_c, recv_before, recv_after,
+):
+    s = lax.axis_index("seg")
+    rank = lax.axis_index("rank")
+    z, core = rank // 2, rank % 2
+    me = s * (2 * CHIP_Z) + rank
+    rows = block_ref.shape[0]
+    half = rows // 2
+    sx = s + 1 - 2 * (s % 2)
+    sy = s + 2 - 4 * (s // 2)
+    sd = sx + sy - s
+    at_x, at_y, at_c = (sx, rank), (sy, rank), (s, rank + 1 - 2 * core)
+    above, below = (s, rank + 2), (s, rank - 2)
+    next_one, prev_one = (s, rank + 1), (s, rank - 1)
+    has_above, has_below = z < CHIP_Z - 1, z > 0
+    has_next, has_prev = rank < 2 * CHIP_Z - 1, rank > 0
+    step_away = (core == 1) & has_next | (core == 0) & has_prev
+    away = (s, rank + 2 * core - 1)
+
+    def number(seg, level):
+        return (seg * CHIP_Z + level) * 2 + core
+
+    def level_of(j):
+        low = z // 2
+        near = jnp.where(j == 0, z, z + 1 - 2 * (z % 2))
+        far = jnp.where(low == 0, j, 3 - j)
+        return jnp.where(j < 2, near, far)
+
+    def remote(src, dst, send, recv, target):
+        return pltpu.make_async_remote_copy(
+            src_ref=src, dst_ref=dst, send_sem=send, recv_sem=recv, device_id=target, device_id_type=MESH
+        )
+
+    def whole(seg, level, send, recv, target):
+        place = held_ref.at[number(seg, level)]
+        return remote(place, place, send, recv, target)
+
+    def up(level):
+        return whole(s, level, send_up.at[level], recv_z.at[level], above)
+
+    def down(level):
+        return whole(s, level, send_down.at[level], recv_z.at[level], below)
+
+    def to_x(level):
+        return whole(s, level, send_x.at[level], recv_x.at[level], at_x)
+
+    def to_y(level):
+        return whole(s, level, send_y.at[level], recv_y.at[level], at_y)
+
+    def half_to_y(level):
+        place = held_ref.at[number(sx, level), pl.ds(0, half)]
+        return remote(place, place, send_dy.at[level], recv_dy.at[level], at_y)
+
+    def half_to_x(level):
+        place = held_ref.at[number(sy, level), pl.ds(half, half)]
+        return remote(place, place, send_dx.at[level], recv_dx.at[level], at_x)
+
+    def to_core(seg, level):
+        chip = seg * CHIP_Z + level
+        return whole(seg, level, send_c.at[chip], recv_c.at[chip], at_c)
+
+    def from_core(chip):
+        place = held_ref.at[chip * 2 + 1 - core]
+        return remote(place, place, send_c.at[chip], recv_c.at[chip], at_c)
+
+    def from_x(level):
+        return whole(sx, level, send_x.at[level], recv_x.at[level], at_x)
+
+    def from_y(level):
+        return whole(sy, level, send_y.at[level], recv_y.at[level], at_y)
+
+    def half_from_y(level):
+        place = held_ref.at[number(sd, level), pl.ds(0, half)]
+        return remote(place, place, send_dy.at[level], recv_dy.at[level], at_y)
+
+    def half_from_x(level):
+        place = held_ref.at[number(sd, level), pl.ds(half, half)]
+        return remote(place, place, send_dx.at[level], recv_dx.at[level], at_x)
+
+    def piece(ref, chip):
+        return ref.at[:, pl.ds(pl.multiple_of(chip * WIDTH, WIDTH), WIDTH)]
+
+    def to_next(chip):
+        return remote(
+            piece(face_ref, chip), piece(before_ref, chip), send_next.at[chip], recv_before.at[chip], next_one
+        )
+
+    def to_prev(chip):
+        return remote(
+            piece(face_ref, chip), piece(after_ref, chip), send_prev.at[chip], recv_after.at[chip], prev_one
+        )
+
+    barrier = pltpu.get_barrier_semaphore()
+
+    def greet(target):
+        pl.semaphore_signal(barrier, inc=1, device_id=target, device_id_type=MESH)
+
+    for target in (at_x, at_y, at_c):
+        greet(target)
+    for present, target in ((has_above, above), (has_below, below), (step_away, away)):
+        pl.when(present)(functools.partial(greet, target))
+    held_ref[me] = block_ref[...]
+    peers = 3 + sum(present.astype(jnp.int32) for present in (has_above, has_below, step_away))
+    pl.semaphore_wait(barrier, peers)
+
+    def spread(level):
+        pl.when(has_above & (level <= z))(lambda: up(level).start())
+        pl.when(has_below & (level >= z))(lambda: down(level).start())
+        to_x(level).start()
+        to_y(level).start()
+        to_core(s, level).start()
+
+    spread(z)
+
+    @pl.when(rank == 0)
+    def _():
+        before_ref[...] = jnp.zeros_like(before_ref)
+
+    @pl.when(rank == 2 * CHIP_Z - 1)
+    def _():
+        after_ref[...] = jnp.zeros_like(after_ref)
+
+    own = me.astype(jnp.float32)
+
+    @pl.loop(0, CHIP_Z + 1)
+    def _(j):
+        @pl.when(j < CHIP_Z - 1)
+        def _():
+            level = level_of(j + 1)
+            whole(s, level, send_up.at[level], recv_z.at[level], at_c).wait_recv()
+            spread(level)
+
+        @pl.when(j < CHIP_Z)
+        def _():
+            level = level_of(j)
+            from_x(level).wait_recv()
+            half_to_y(level).start()
+            to_core(sx, level).start()
+            from_y(level).wait_recv()
+            half_to_x(level).start()
+            to_core(sy, level).start()
+
+        @pl.loop(0, 4)
+        def _(q):
+            level = level_of(jnp.where(q < 3, j, j - 1))
+            seg = jnp.where(q == 0, s, jnp.where(q == 1, sx, jnp.where(q == 2, sy, sd)))
+            chip = seg * CHIP_Z + level
+
+            @pl.when((q == 3) & (j > 0))
+            def _():
+                half_from_x(level).wait_recv()
+                half_from_y(level).wait_recv()
+                to_core(sd, level).start()
+
+            @pl.when(((q == 3) & (j > 0)) | ((q < 3) & (j < CHIP_Z)))
+            def _():
+                from_core(chip).wait_recv()
+                gathered, octants = [], []
+                for c in range(2):
+                    block = held_ref[chip * 2 + c]
+                    mask = jnp.where(block[OWNERS:, :] == own, 1.0, 0.0)
+                    held, octant = chosen_children(block[:OWNERS, :], keys_of(mask, earlier_ref[...]), WIDTH // 2)
+                    gathered.append(held)
+                    octants.append(octant)
+                mass, face = masses(
+                    jnp.concatenate(gathered, axis=1), jnp.concatenate(octants, axis=1), a1_ref, a2_ref, a3_ref, ad_ref
+                )
+                lanes = pl.ds(pl.multiple_of(chip * WIDTH, WIDTH), WIDTH)
+                mass_ref[:, lanes] = mass
+                face_ref[:, lanes] = face
+                pl.when(has_next)(lambda: to_next(chip).start())
+                pl.when(has_prev)(lambda: to_prev(chip).start())
+
+    @pl.loop(0, CHIP_Z)
+    def _(level):
+        pl.when(has_above & (level <= z))(lambda: up(level).wait_send())
+        pl.when(has_below & (level >= z))(lambda: down(level).wait_send())
+        to_x(level).wait_send()
+        to_y(level).wait_send()
+        half_to_x(level).wait_send()
+        half_to_y(level).wait_send()
+
+    @pl.loop(0, 4 * CHIP_Z)
+    def _(chip):
+        to_core(chip // CHIP_Z, chip % CHIP_Z).wait_send()
+
+        @pl.when(has_next)
+        def _():
+            to_next(chip).wait_send()
+            remote(
+                piece(face_ref, chip), piece(after_ref, chip), send_next.at[chip], recv_after.at[chip], next_one
+            ).wait_recv()
+
+        @pl.when(has_prev)
+        def _():
+            to_prev(chip).wait_send()
+            remote(
+                piece(face_ref, chip), piece(before_ref, chip), send_prev.at[chip], recv_before.at[chip], prev_one
+            ).wait_recv()
+
+
+def gather_and_compute(block, tables, cap):
+    devices = 8 * CHIP_Z
+    slots = devices * cap
+    vmem = pl.BlockSpec(memory_space=pltpu.VMEM)
+    faces = jax.ShapeDtypeStruct((152, slots), jnp.float32)
+    dma = pltpu.SemaphoreType.DMA
+    chips = 4 * CHIP_Z
+    return pl.pallas_call(
+        gather_kernel,
+        in_specs=[vmem] * (1 + len(tables)),
+        out_specs=[vmem] * 4,
+        out_shape=[jax.ShapeDtypeStruct((125, slots), jnp.float32), faces, faces, faces],
+        scratch_shapes=[pltpu.VMEM((devices,) + block.shape, jnp.float32)]
+        + [dma((CHIP_Z,))] * 6
+        + [dma((chips,))] * 3
+        + [dma((CHIP_Z,))] * 5
+        + [dma((chips,))] * 3,
+        compiler_params=pltpu.CompilerParams(
+            collective_id=0, has_side_effects=True, vmem_limit_bytes=48 * 1024 * 1024
+        ),
+        name="gather_and_compute",
+    )(block, *tables)
 
 
 def assemble_kernel(link_ref, before_ref, own_ref, after_ref, out_ref, low_ref, high_ref, row_low, row_high):
@@ -312,11 +558,14 @@
     )
     owners = child_owner.reshape(kids // 8, 8).T.astype(jnp.float32)
     block = jnp.concatenate([coords, owners], axis=0)
-    blocks = lax.all_gather(block, ("seg", "rank"))
-    mask = (blocks[:, OWNERS:, :] == me.astype(jnp.float32)).astype(jnp.float32)
-    mass, faces = geometry(blocks, mask.reshape(devices * 8, kids // 8), tables, cap)
-    before = shifted(faces, "rank", 1)
-    after = shifted(faces, "rank", -1)
+    if lax.axis_size("seg") == 4 and lax.axis_size("rank") == 2 * CHIP_Z and 2 * cap == WIDTH:
+        mass, faces, before, after = gather_and_compute(block, tables, cap)
+    else:
+        blocks = lax.all_gather(block, ("seg", "rank"))
+        mask = (blocks[:, OWNERS:, :] == me.astype(jnp.float32)).astype(jnp.float32)
+        mass, faces = geometry(blocks, mask, tables, cap)
+        before = shifted(faces, "rank", 1)
+        after = shifted(faces, "rank", -1)
     return (mass, assemble(face_link.T.reshape(-1), before, faces, after))
 
 

time: 225 us -> 131 us (0.58)
  waiting for transfers between devices: 118 us -> 0 us
  Pallas kernels: 73.6 us -> 114 us
  between operations: 14.2 us -> 0.75 us
  starting transfers between devices: 5.8 us -> 0 us
  local copies, waits for them, and re-layouts: 10 us -> 13 us
    all_gather x1 -> x0, waiting for transfers between devices: 89.5 us -> none  [body(): blocks = lax.all_gather(block, ('seg', 'rank'))]
    pallas_call x1, Pallas kernels: 35.9 us -> 76.9 us  [gather_and_compute(): pl.pallas_call(gather_kernel, in_specs=[vmem] * (1 + len(tables)), out_sp...]
    ppermute x2 -> x0, waiting for transfers between devices: 28.9 us -> none  [shifted(): return lax.ppermute(array, axis, pairs)]
    ppermute x2 -> x0, starting transfers between devices: 5.76 us -> none  [shifted(): return lax.ppermute(array, axis, pairs)]
    unnamed x17 -> x16, local copies, waits for them, and re-layouts: 6.45 us -> 8.55 us
  transfers between devices with their start and end apart: 3 -> 0, of which waited for: 3 -> 0; matrix products, arithmetic and copies ran while one was open for 0% -> 0% of each run, Pallas kernels for 0% -> 0%
where the time goes in v2:
time: 131 us; the launch traced here: 130 us
  Pallas kernels  114 us (87%)
  local copies, waits for them, and re-layouts  13 us (10%)
  other arithmetic  1.43 us (1%)
    pallas_call x1, Pallas kernels, gather_and_compute(): pl.pallas_call(gather_kernel, in_specs=[vmem] * (1 + len(tables)), out_sp...  76.9 us
    pallas_call x1, Pallas kernels, assemble(): pl.pallas_call(assemble_kernel, in_specs=[pl.BlockSpec(memory_space=pltpu...  37.4 us
    unnamed x16, local copies, waits for them, and re-layouts  8.55 us
    gather x1, local copies, waits for them, and re-layouts, body(): picked = parent_nodes[marks[0]]  3.37 us

profile of v2, /device:TPU:1, one launch (start us, length us, event | category | flops | bytes accessed | tf_op | source)
XLA Modules:
  0.0 130.2 jit_solution(12006776882232911564)
XLA Ops:
  0.6 0.7 compare_select_fusion
  1.3 0.7 convert_reduce_fusion
  2.0 1.0 reshape.37.link_ref
  3.0 0.1 convert_element_type.10
  3.1 0.1 copy.14
  3.2 5.5 %copy.13 = f32[2560,375]{1,0:T(8,128)} copy(f32[2560,375]{0,1:T(8,128)} %param.10) | data formatting | bytes 7680000 | tf_op args[0]
  8.7 0.0 copy-start.6
  8.7 0.0 copy-start.1
  8.7 0.0 copy-start.2
  8.7 0.0 copy-start.3
  8.7 0.0 copy-start.4
  8.7 0.0 copy-start.5
  8.7 3.4 %gather_fusion = f32[256,375]{1,0:T(8,128)S(1)} fusion(f32[2560,375]{1,0:T(8,128)} %copy.13, s32[1024]{0:T(1024)S(1)} %pad_clamp_fusion), kind=kCustom, calls=%fused_computation | custom fusion | bytes 769024 | tf_op jit(solution)/shard_map/gather | solution.py:551
  12.1 0.0 copy-done.6
  12.1 0.7 fusion
  12.8 0.0 copy-done.1
  12.8 0.0 copy-done.2
  12.8 0.0 copy-done.3
  12.8 0.0 copy-done.4
  12.9 0.0 copy-done.5
  12.9 76.9 %gather_and_compute.1 = (f32[125,4096]{1,0:T(8,128)S(1)}, f32[152,4096]{1,0:T(8,128)S(1)}, f32[152,4096]{1,0:T(8,128)}, f32[152,4096]{1,0:T(8,128)}) custom-call(f32[320,256]{1,0:T(8,128)S(1)} %pad_maximum_fusion.block_ref, bf16[256,256]{1,0:T(8,128)(2,1)S(1)} %copy-done.5, bf16[256,312]{1,0:T(8,128)(2,1)S(1)} %copy-done.4, bf16[256,384]{1,0:T(8,128)(2,1)S(1)} %copy-done.3, ...), custom_call_target="tpu_custom_call" | custom-call | tf_op jit(solution)/shard_map/gather_and_compute/pallas_call | solution.py:472
  89.8 0.0 copy-start
  89.8 1.7 %copy-done = f32[152,4096]{1,0:T(8,128)S(1)} copy-done((f32[152,4096]{1,0:T(8,128)S(1)}, f32[152,4096]{1,0:T(8,128)}, u32[]{:S(2)}) %copy-start) | copy-done | bytes 2490392
  91.5 37.4 %assemble.1 = f32[150,4096]{1,0:T(8,128)} custom-call(s32[24576]{0:T(1024)S(1)} %reshape.37.link_ref, f32[152,4096]{1,0:T(8,128)S(1)} %copy-done, f32[152,4096]{1,0:T(8,128)S(1)} %get-tuple-element.8.own_ref, f32[152,4096]{1,0:T(8,128)} %get-tuple-element.9.after_ref), custom_call_target="tpu_custom_call" | custom-call | tf_op jit(solution)/shard_map/assemble/pallas_call | solution.py:529
  128.9 1.3 %copy.16 = f32[125,4096]{1,0:T(8,128)} copy(f32[125,4096]{1,0:T(8,128)S(1)} %get-tuple-element.12) | data formatting | bytes 4096000
  (2 shorter events, 0.0 us)
Async XLA Ops:
  8.7 3.4 %copy-start.6 = (f32[312,375]{1,0:T(8,128)S(1)}, f32[312,375]{1,0:T(8,128)}, u32[]{:S(2)}) copy-start(f32[312,375]{1,0:T(8,128)} %constant.21.clone) | copy-start | bytes 1404004
  8.7 4.1 %copy-start.1 = (bf16[688,384]{1,0:T(8,128)(2,1)S(1)}, bf16[688,384]{1,0:T(8,128)(2,1)}, u32[]{:S(2)}) copy-start(bf16[688,384]{1,0:T(8,128)(2,1)} %constant.20.clone.ad_ref) | copy-start | bytes 1585156
  8.7 4.1 %copy-start.2 = (bf16[256,384]{1,0:T(8,128)(2,1)S(1)}, bf16[256,384]{1,0:T(8,128)(2,1)}, u32[]{:S(2)}) copy-start(bf16[256,384]{1,0:T(8,128)(2,1)} %constant.19.clone.a3_ref) | copy-start | bytes 589828
  8.7 4.2 %copy-start.3 = (bf16[256,384]{1,0:T(8,128)(2,1)S(1)}, bf16[256,384]{1,0:T(8,128)(2,1)}, u32[]{:S(2)}) copy-start(bf16[256,384]{1,0:T(8,128)(2,1)} %constant.18.clone.a2_ref) | copy-start | bytes 589828
  8.7 4.2 %copy-start.4 = (bf16[256,312]{1,0:T(8,128)(2,1)S(1)}, bf16[256,312]{1,0:T(8,128)(2,1)}, u32[]{:S(2)}) copy-start(bf16[256,312]{1,0:T(8,128)(2,1)} %constant.17.clone.a1_ref) | copy-start | bytes 479236
  8.7 4.2 %copy-start.5 = (bf16[256,256]{1,0:T(8,128)(2,1)S(1)}, bf16[256,256]{1,0:T(8,128)(2,1)}, u32[]{:S(2)}) copy-start(bf16[256,256]{1,0:T(8,128)(2,1)} %constant.16.clone.earlier_ref) | copy-start | bytes 393220
  89.8 1.7 %copy-start = (f32[152,4096]{1,0:T(8,128)S(1)}, f32[152,4096]{1,0:T(8,128)}, u32[]{:S(2)}) copy-start(f32[152,4096]{1,0:T(8,128)} %get-tuple-element.7.before_ref) | copy-start | bytes 7471108

commit v3 on v2

--- a/solution.py
+++ b/solution.py
@@ -253,12 +253,26 @@
     )(blocks, mask, *tables)
 
 
+def picked_coords(nodes, marks, pick):
+    f32 = jnp.float32
+    row = lax.broadcasted_iota(jnp.int32, (nodes.shape[1], marks.shape[1]), 0)
+    chosen = jnp.where(row == marks, 1.0, 0.0).astype(jnp.bfloat16)
+    coords = None
+    for _ in range(3):
+        part = nodes.astype(jnp.bfloat16)
+        nodes = nodes - part.astype(f32)
+        part = jnp.dot(part, chosen, preferred_element_type=f32).astype(jnp.bfloat16)
+        part = jnp.dot(pick, part, preferred_element_type=f32)
+        coords = part if coords is None else coords + part
+    return coords
+
+
 MESH = pl.DeviceIdType.MESH
 CHIP_Z = 4
 
 
 def gather_kernel(
-    block_ref, earlier_ref, a1_ref, a2_ref, a3_ref, ad_ref,
+    nodes_ref, marks_ref, owners_ref, pick_ref, earlier_ref, a1_ref, a2_ref, a3_ref, ad_ref,
     mass_ref, face_ref, before_ref, after_ref, held_ref,
     send_up, send_down, send_x, send_y, send_dx, send_dy, send_c, send_next, send_prev,
     recv_z, recv_x, recv_y, recv_dx, recv_dy, recv_c, recv_before, recv_after,
@@ -267,8 +281,7 @@
     rank = lax.axis_index("rank")
     z, core = rank // 2, rank % 2
     me = s * (2 * CHIP_Z) + rank
-    rows = block_ref.shape[0]
-    half = rows // 2
+    half = held_ref.shape[1] // 2
     sx = s + 1 - 2 * (s % 2)
     sy = s + 2 - 4 * (s // 2)
     sd = sx + sy - s
@@ -362,7 +375,8 @@
         greet(target)
     for present, target in ((has_above, above), (has_below, below), (step_away, away)):
         pl.when(present)(functools.partial(greet, target))
-    held_ref[me] = block_ref[...]
+    held_ref[me, :OWNERS, :] = picked_coords(nodes_ref[...], marks_ref[...], pick_ref[...])
+    held_ref[me, OWNERS:, :] = owners_ref[...]
     peers = 3 + sum(present.astype(jnp.int32) for present in (has_above, has_below, step_away))
     pl.semaphore_wait(barrier, peers)
 
@@ -385,16 +399,26 @@
 
     own = me.astype(jnp.float32)
 
-    @pl.loop(0, CHIP_Z + 1)
-    def _(j):
-        @pl.when(j < CHIP_Z - 1)
+    def along_z(position):
+        level = level_of(position)
+        whole(s, level, send_up.at[level], recv_z.at[level], at_c).wait_recv()
+        spread(level)
+
+    def diagonal(level):
+        half_from_x(level).wait_recv()
+        half_from_y(level).wait_recv()
+        to_core(sd, level).start()
+
+    middle = (has_above & has_below).astype(jnp.int32)
+
+    @pl.loop(0, 4 * CHIP_Z + 2)
+    def _(t):
+        j, k = (t + 3) // 4 - 1, (t + 3) % 4
+
+        @pl.when((k == 0) & (j >= 0) & (j < CHIP_Z))
         def _():
-            level = level_of(j + 1)
-            whole(s, level, send_up.at[level], recv_z.at[level], at_c).wait_recv()
-            spread(level)
-
-        @pl.when(j < CHIP_Z)
-        def _():
+            pl.when((middle == 1) & (j == 0))(lambda: along_z(1))
+            pl.when(j + 1 + middle < CHIP_Z)(lambda: along_z(j + 1 + middle))
             level = level_of(j)
             from_x(level).wait_recv()
             half_to_y(level).start()
@@ -403,36 +427,32 @@
             half_to_x(level).start()
             to_core(sy, level).start()
 
-        @pl.loop(0, 4)
-        def _(q):
-            level = level_of(jnp.where(q < 3, j, j - 1))
-            seg = jnp.where(q == 0, s, jnp.where(q == 1, sx, jnp.where(q == 2, sy, sd)))
-            chip = seg * CHIP_Z + level
-
-            @pl.when((q == 3) & (j > 0))
-            def _():
-                half_from_x(level).wait_recv()
-                half_from_y(level).wait_recv()
-                to_core(sd, level).start()
-
-            @pl.when(((q == 3) & (j > 0)) | ((q < 3) & (j < CHIP_Z)))
-            def _():
-                from_core(chip).wait_recv()
-                gathered, octants = [], []
-                for c in range(2):
-                    block = held_ref[chip * 2 + c]
-                    mask = jnp.where(block[OWNERS:, :] == own, 1.0, 0.0)
-                    held, octant = chosen_children(block[:OWNERS, :], keys_of(mask, earlier_ref[...]), WIDTH // 2)
-                    gathered.append(held)
-                    octants.append(octant)
-                mass, face = masses(
-                    jnp.concatenate(gathered, axis=1), jnp.concatenate(octants, axis=1), a1_ref, a2_ref, a3_ref, ad_ref
-                )
-                lanes = pl.ds(pl.multiple_of(chip * WIDTH, WIDTH), WIDTH)
-                mass_ref[:, lanes] = mass
-                face_ref[:, lanes] = face
-                pl.when(has_next)(lambda: to_next(chip).start())
-                pl.when(has_prev)(lambda: to_prev(chip).start())
+        pl.when((k == 2) & (j >= 1) & (j < CHIP_Z))(lambda: diagonal(level_of(j - 1)))
+        pl.when(t == 4 * CHIP_Z + 1)(lambda: diagonal(level_of(CHIP_Z - 1)))
+        column = (k == 0) & (j < CHIP_Z - 1) | (t == 0)
+        slanted = (k == 3) & (j >= 1) | (t == 4 * CHIP_Z + 1)
+        position = jnp.where(t == 0, 0, jnp.where(column, j + 1, jnp.where(slanted, j - 1, j)))
+        seg = jnp.where(column, s, jnp.where(slanted, sd, jnp.where(k == 1, sx, sy)))
+        chip = seg * CHIP_Z + level_of(position)
+
+        @pl.when(column | slanted | (k == 1) | (k == 2))
+        def _():
+            from_core(chip).wait_recv()
+            gathered, octants = [], []
+            for c in range(2):
+                block = held_ref[chip * 2 + c]
+                mask = jnp.where(block[OWNERS:, :] == own, 1.0, 0.0)
+                held, octant = chosen_children(block[:OWNERS, :], keys_of(mask, earlier_ref[...]), WIDTH // 2)
+                gathered.append(held)
+                octants.append(octant)
+            mass, face = masses(
+                jnp.concatenate(gathered, axis=1), jnp.concatenate(octants, axis=1), a1_ref, a2_ref, a3_ref, ad_ref
+            )
+            lanes = pl.ds(pl.multiple_of(chip * WIDTH, WIDTH), WIDTH)
+            mass_ref[:, lanes] = mass
+            face_ref[:, lanes] = face
+            pl.when(has_next)(lambda: to_next(chip).start())
+            pl.when(has_prev)(lambda: to_prev(chip).start())
 
     @pl.loop(0, CHIP_Z)
     def _(level):
@@ -462,7 +482,7 @@
             ).wait_recv()
 
 
-def gather_and_compute(block, tables, cap):
+def gather_and_compute(nodes, marks, owners, pick, tables, cap):
     devices = 8 * CHIP_Z
     slots = devices * cap
     vmem = pl.BlockSpec(memory_space=pltpu.VMEM)
@@ -471,10 +491,10 @@
     chips = 4 * CHIP_Z
     return pl.pallas_call(
         gather_kernel,
-        in_specs=[vmem] * (1 + len(tables)),
+        in_specs=[vmem] * (4 + len(tables)),
         out_specs=[vmem] * 4,
         out_shape=[jax.ShapeDtypeStruct((125, slots), jnp.float32), faces, faces, faces],
-        scratch_shapes=[pltpu.VMEM((devices,) + block.shape, jnp.float32)]
+        scratch_shapes=[pltpu.VMEM((devices, OWNERS + 8, owners.shape[1]), jnp.float32)]
         + [dma((CHIP_Z,))] * 6
         + [dma((chips,))] * 3
         + [dma((CHIP_Z,))] * 5
@@ -483,7 +503,7 @@
             collective_id=0, has_side_effects=True, vmem_limit_bytes=48 * 1024 * 1024
         ),
         name="gather_and_compute",
-    )(block, *tables)
+    )(nodes, marks, owners, pick, *tables)
 
 
 def assemble_kernel(link_ref, before_ref, own_ref, after_ref, out_ref, low_ref, high_ref, row_low, row_high):
@@ -548,20 +568,20 @@
     me = lax.axis_index("seg") * lax.axis_size("rank") + lax.axis_index("rank")
     kids = child_owner.shape[0]
     cap = max(2, 2 * kids // devices)
-    picked = parent_nodes[marks[0]]
-    coords = lax.dot_general(
-        jnp.asarray(pick, jnp.float32),
-        picked,
-        NT,
-        precision=lax.Precision.HIGHEST,
-        preferred_element_type=jnp.float32,
-    )
     owners = child_owner.reshape(kids // 8, 8).T.astype(jnp.float32)
-    block = jnp.concatenate([coords, owners], axis=0)
     if lax.axis_size("seg") == 4 and lax.axis_size("rank") == 2 * CHIP_Z and 2 * cap == WIDTH:
-        mass, faces, before, after = gather_and_compute(block, tables, cap)
+        mass, faces, before, after = gather_and_compute(
+            parent_nodes.T, marks, owners, jnp.asarray(pick, jnp.bfloat16), tables, cap
+        )
     else:
-        blocks = lax.all_gather(block, ("seg", "rank"))
+        coords = lax.dot_general(
+            jnp.asarray(pick, jnp.float32),
+            parent_nodes[marks[0]],
+            NT,
+            precision=lax.Precision.HIGHEST,
+            preferred_element_type=jnp.float32,
+        )
+        blocks = lax.all_gather(jnp.concatenate([coords, owners], axis=0), ("seg", "rank"))
         mask = (blocks[:, OWNERS:, :] == me.astype(jnp.float32)).astype(jnp.float32)
         mass, faces = geometry(blocks, mask, tables, cap)
         before = shifted(faces, "rank", 1)

time: 131 us -> 121 us (0.924)
  Pallas kernels: 114 us -> 109 us
  local copies, waits for them, and re-layouts: 13 us -> 10.5 us
    pallas_call x1, Pallas kernels: 76.9 us -> 71.2 us  [gather_and_compute(): pl.pallas_call(gather_kernel, in_specs=[vmem] * (4 + len(tables)), out_sp...]
    gather x1 -> x0, local copies, waits for them, and re-layouts: 3.37 us -> none  [body(): picked = parent_nodes[marks[0]]]
    unnamed x16 -> x17, local copies, waits for them, and re-layouts: 8.55 us -> 9.37 us
where the time goes in v3:
time: 121 us; the launch traced here: 120 us
  Pallas kernels  109 us (90%)
  local copies, waits for them, and re-layouts  10.5 us (9%)
    pallas_call x1, Pallas kernels, gather_and_compute(): pl.pallas_call(gather_kernel, in_specs=[vmem] * (4 + len(tables)), out_sp...  71.2 us
    pallas_call x1, Pallas kernels, assemble(): pl.pallas_call(assemble_kernel, in_specs=[pl.BlockSpec(memory_space=pltpu...  37.4 us
    unnamed x17, local copies, waits for them, and re-layouts  9.37 us

profile of v3, /device:TPU:1, one launch (start us, length us, event | category | flops | bytes accessed | tf_op | source)
XLA Modules:
  0.0 120.4 jit_solution(13497038424525997361)
XLA Ops:
  0.6 0.7 convert_reduce_fusion
  1.4 1.0 reshape.9.link_ref
  2.3 0.1 convert_element_type.8
  2.4 0.1 copy.12
  2.5 0.0 copy-start.1
  2.5 1.1 copy-done.1
  3.5 0.0 copy-start.2
  3.5 0.9 copy-done.2
  4.5 0.0 copy-start.3
  4.5 0.9 copy-done.3
  5.4 0.0 copy-start.4
  5.4 0.9 copy-done.4
  6.3 0.0 copy-start.5
  6.3 0.9 copy-done.5
  7.3 0.0 copy-start.6
  7.3 0.9 copy-done.6
  8.2 0.0 copy-start.7
  8.2 0.7 copy-done.7
  8.8 71.2 %gather_and_compute.1 = (f32[125,4096]{1,0:T(8,128)S(1)}, f32[152,4096]{1,0:T(8,128)S(1)}, f32[152,4096]{1,0:T(8,128)}, f32[152,4096]{1,0:T(8,128)}) custom-call(f32[375,2560]{1,0:T(8,128)} %bitcast.4, s32[1,256]{1,0:T(1,128)S(1)} %copy-done.7, f32[8,256]{1,0:T(8,128)S(1)} %bitcast.3, bf16[312,375]{1,0:T(8,128)(2,1)S(1)} %copy-done.2, ...), custom_call_target="tpu_custom_call" | custom-call | tf_op jit(solution)/shard_map/gather_and_compute/pallas_call | solution.py:492
  80.0 0.0 copy-start
  80.0 1.7 %copy-done = f32[152,4096]{1,0:T(8,128)S(1)} copy-done((f32[152,4096]{1,0:T(8,128)S(1)}, f32[152,4096]{1,0:T(8,128)}, u32[]{:S(2)}) %copy-start) | copy-done | bytes 2490392
  81.7 37.4 %assemble.1 = f32[150,4096]{1,0:T(8,128)} custom-call(s32[24576]{0:T(1024)S(1)} %reshape.9.link_ref, f32[152,4096]{1,0:T(8,128)S(1)} %copy-done, f32[152,4096]{1,0:T(8,128)S(1)} %get-tuple-element.8.own_ref, f32[152,4096]{1,0:T(8,128)} %get-tuple-element.9.after_ref), custom_call_target="tpu_custom_call" | custom-call | tf_op jit(solution)/shard_map/assemble/pallas_call | solution.py:549
  119.1 1.3 %copy.14 = f32[125,4096]{1,0:T(8,128)} copy(f32[125,4096]{1,0:T(8,128)S(1)} %get-tuple-element.12) | data formatting | bytes 4096000
Async XLA Ops:
  2.5 1.1 copy-start.1
  3.5 0.9 copy-start.2
  4.5 0.9 copy-start.3
  5.4 0.9 copy-start.4
  6.3 0.9 copy-start.5
  7.3 0.9 copy-start.6
  8.2 0.7 copy-start.7
  80.0 1.7 %copy-start = (f32[152,4096]{1,0:T(8,128)S(1)}, f32[152,4096]{1,0:T(8,128)}, u32[]{:S(2)}) copy-start(f32[152,4096]{1,0:T(8,128)} %get-tuple-element.7.before_ref) | copy-start | bytes 7471108

commit v4 on v3

--- a/solution.py
+++ b/solution.py
@@ -101,12 +101,18 @@
 OWNERS = 3 * HELD
 WIDTH = 256
 NT = (((1,), (1,)), ((), ()))
+FACES = 160
+STRIP = 32
+SIDES = (0, 256, 512)
+DERIVS = 768
+EARLIER = DERIVS + 384 + 2 * FACES
+PICK = EARLIER + 256
 
 
 def parts_of(table):
     high = table.astype(ml_dtypes.bfloat16)
     low = (table - high.astype(np.float64)).astype(ml_dtypes.bfloat16)
-    return jnp.asarray(np.concatenate([high, high, low], axis=1))
+    return np.concatenate([high, high, low], axis=1)
 
 
 def padded(table, rows, columns):
@@ -130,9 +136,12 @@
     rows += [padded(derivs[d], 128, 128) for d in (1, 2)]
     along = [derivs[tangents[f][0]][nodes[f]] * face_weights[:, None] for f in range(6)]
     across = [derivs[tangents[f][1]][nodes[f]] for f in range(6)]
-    rows += [padded(np.concatenate(part), 152, 128) for part in (along, across)]
-    earlier = jnp.asarray(np.triu(np.ones((256, 256)), 1).astype(ml_dtypes.bfloat16))
-    return pick, [earlier] + [parts_of(table) for table in (first, second, third, np.concatenate(rows))]
+    for part in (along, across):
+        rows += [padded(np.concatenate(part[:5]), 128, 128), padded(part[5], 32, 128)]
+    earlier = np.triu(np.ones((256, 256)), 1)
+    tables = [parts_of(table) for table in (first, second, third, np.concatenate(rows))] + [earlier, pick]
+    tables = [padded(table.astype(np.float64), table.shape[0], 384) for table in tables]
+    return pick, jnp.asarray(np.concatenate(tables).astype(ml_dtypes.bfloat16))
 
 
 def stacked(values):
@@ -166,18 +175,19 @@
     return held, octant
 
 
-def masses(held, octant, a1_ref, a2_ref, a3_ref, ad_ref):
+def masses(held, octant, table_ref):
     f32 = jnp.float32
     bits = octant_bits(octant[0:1, :])
     high = jnp.concatenate([held[c * HELD : (c + 1) * HELD] for c in range(3)], axis=1)
     low = jnp.concatenate([held[(c + 3) * HELD : (c + 4) * HELD] for c in range(3)], axis=1)
     operand = jnp.concatenate([high, low, high], axis=0).astype(jnp.bfloat16)
-    for table_ref, bit in zip((a1_ref, a2_ref, a3_ref), bits):
-        sides = jnp.dot(table_ref[...], operand, preferred_element_type=f32)
+    for start, bit in zip(SIDES, bits):
+        table = table_ref[start : start + 256, : operand.shape[0]]
+        sides = jnp.dot(table, operand, preferred_element_type=f32)
         operand = stacked(jnp.where(bit > 0.5, sides[128:], sides[:128]))
 
     def components(start, rows):
-        table = ad_ref[start : start + rows, :]
+        table = table_ref[DERIVS + start : DERIVS + start + rows, :]
         values = jnp.dot(table, operand, preferred_element_type=f32)
         return [values[:, c * WIDTH : (c + 1) * WIDTH] for c in range(3)]
 
@@ -187,7 +197,7 @@
     first, second, third = (components(128 * d, 128) for d in range(3))
     normal = crossed(second, third)
     mass = (first[0] * normal[0] + first[1] * normal[1] + first[2] * normal[2])[:125]
-    normal = crossed(components(384, 152), components(536, 152))
+    normal = crossed(components(384, FACES), components(384 + FACES, FACES))
     face = jnp.sqrt(normal[0] * normal[0] + normal[1] * normal[1] + normal[2] * normal[2])
     return mass, face
 
@@ -203,11 +213,11 @@
     return keys
 
 
-def geometry_kernel(cap, block_ref, mask_ref, earlier_ref, a1_ref, a2_ref, a3_ref, ad_ref, mass_ref, face_ref):
+def geometry_kernel(cap, block_ref, mask_ref, table_ref, mass_ref, face_ref):
     gathered, octants = [], []
     aligned = cap % 128 == 0
     for s in range(WIDTH // cap):
-        keys = keys_of(mask_ref[s], earlier_ref[...])
+        keys = keys_of(mask_ref[s], table_ref[EARLIER : EARLIER + 256, :256])
         if not aligned:
             keys = [key + float(s * cap) for key in keys]
         held, octant = chosen_children(block_ref[s, :OWNERS, :], keys, cap if aligned else WIDTH)
@@ -219,7 +229,7 @@
     else:
         held = sum(gathered[1:], gathered[0])
         octant = sum(octants[1:], octants[0])
-    mass, face = masses(held, octant, a1_ref, a2_ref, a3_ref, ad_ref)
+    mass, face = masses(held, octant, table_ref)
     mass_ref[...] = mass
     face_ref[...] = face
 
@@ -238,19 +248,19 @@
         in_specs=[
             pl.BlockSpec((group,) + blocks.shape[1:], lambda i: (i, 0, 0)),
             pl.BlockSpec((group,) + mask.shape[1:], lambda i: (i, 0, 0)),
-        ]
-        + [whole_spec(table) for table in tables],
+            whole_spec(tables),
+        ],
         out_specs=[
             pl.BlockSpec((125, WIDTH), lambda i: (0, i)),
-            pl.BlockSpec((152, WIDTH), lambda i: (0, i)),
+            pl.BlockSpec((FACES, WIDTH), lambda i: (0, i)),
         ],
         out_shape=[
             jax.ShapeDtypeStruct((125, slots), jnp.float32),
-            jax.ShapeDtypeStruct((152, slots), jnp.float32),
+            jax.ShapeDtypeStruct((FACES, slots), jnp.float32),
         ],
         compiler_params=pltpu.CompilerParams(vmem_limit_bytes=48 * 1024 * 1024),
         name="geometry",
-    )(blocks, mask, *tables)
+    )(blocks, mask, tables)
 
 
 def picked_coords(nodes, marks, pick):
@@ -268,14 +278,15 @@
 
 
 MESH = pl.DeviceIdType.MESH
+DELAY = 5
 CHIP_Z = 4
 
 
 def gather_kernel(
-    nodes_ref, marks_ref, owners_ref, pick_ref, earlier_ref, a1_ref, a2_ref, a3_ref, ad_ref,
-    mass_ref, face_ref, before_ref, after_ref, held_ref,
-    send_up, send_down, send_x, send_y, send_dx, send_dy, send_c, send_next, send_prev,
-    recv_z, recv_x, recv_y, recv_dx, recv_dy, recv_c, recv_before, recv_after,
+    nodes_ref, marks_ref, owners_ref, table_ref,
+    mass_ref, face_ref, low_ref, before_ref, after_ref, held_ref,
+    send_up, send_down, send_x, send_y, send_dx, send_dy, send_c, send_next, send_prev, send_low_next, send_low_prev,
+    recv_z, recv_x, recv_y, recv_dx, recv_dy, recv_c, recv_before, recv_after, recv_low_before, recv_low_after,
 ):
     s = lax.axis_index("seg")
     rank = lax.axis_index("rank")
@@ -353,18 +364,65 @@
         place = held_ref.at[number(sd, level), pl.ds(half, half)]
         return remote(place, place, send_dx.at[level], recv_dx.at[level], at_x)
 
-    def piece(ref, chip):
-        return ref.at[:, pl.ds(pl.multiple_of(chip * WIDTH, WIDTH), WIDTH)]
+    slots = face_ref.shape[1]
+
+    def strip(ref, chip):
+        rows = pl.ds(ref.shape[0] - STRIP, STRIP)
+        return ref.at[rows, pl.ds(pl.multiple_of(chip * WIDTH, WIDTH), WIDTH)]
+
+    def part(number, chip):
+        return low_ref.at[pl.ds(pl.multiple_of(number * slots + chip * WIDTH, WIDTH), WIDTH)]
 
     def to_next(chip):
-        return remote(
-            piece(face_ref, chip), piece(before_ref, chip), send_next.at[chip], recv_before.at[chip], next_one
-        )
+        return [
+            remote(
+                strip(face_ref, chip), strip(before_ref, chip), send_next.at[chip], recv_before.at[chip], next_one
+            ),
+            remote(
+                part(1, chip), part(0, chip), send_low_next.at[chip], recv_low_before.at[chip], next_one
+            ),
+        ]
 
     def to_prev(chip):
-        return remote(
-            piece(face_ref, chip), piece(after_ref, chip), send_prev.at[chip], recv_after.at[chip], prev_one
-        )
+        return [
+            remote(
+                strip(face_ref, chip), strip(after_ref, chip), send_prev.at[chip], recv_after.at[chip], prev_one
+            ),
+            remote(
+                part(1, chip), part(2, chip), send_low_prev.at[chip], recv_low_after.at[chip], prev_one
+            ),
+        ]
+
+    def from_prev(chip):
+        return [
+            remote(
+                strip(face_ref, chip), strip(before_ref, chip), send_prev.at[chip], recv_before.at[chip], prev_one
+            ),
+            remote(
+                part(1, chip), part(0, chip), send_low_prev.at[chip], recv_low_before.at[chip], prev_one
+            ),
+        ]
+
+    def from_next(chip):
+        return [
+            remote(
+                strip(face_ref, chip), strip(after_ref, chip), send_next.at[chip], recv_after.at[chip], next_one
+            ),
+            remote(
+                part(1, chip), part(2, chip), send_low_next.at[chip], recv_low_after.at[chip], next_one
+            ),
+        ]
+
+    def send_faces(chip):
+        @pl.when(has_next)
+        def _():
+            for copy in to_next(chip):
+                copy.start()
+
+        @pl.when(has_prev)
+        def _():
+            for copy in to_prev(chip):
+                copy.start()
 
     barrier = pltpu.get_barrier_semaphore()
 
@@ -375,7 +433,7 @@
         greet(target)
     for present, target in ((has_above, above), (has_below, below), (step_away, away)):
         pl.when(present)(functools.partial(greet, target))
-    held_ref[me, :OWNERS, :] = picked_coords(nodes_ref[...], marks_ref[...], pick_ref[...])
+    held_ref[me, :OWNERS, :] = picked_coords(nodes_ref[...], marks_ref[...], table_ref[PICK : PICK + OWNERS, :375])
     held_ref[me, OWNERS:, :] = owners_ref[...]
     peers = 3 + sum(present.astype(jnp.int32) for present in (has_above, has_below, step_away))
     pl.semaphore_wait(barrier, peers)
@@ -392,10 +450,12 @@
     @pl.when(rank == 0)
     def _():
         before_ref[...] = jnp.zeros_like(before_ref)
+        low_ref[:slots, :] = jnp.zeros((slots, 128), jnp.float32)
 
     @pl.when(rank == 2 * CHIP_Z - 1)
     def _():
         after_ref[...] = jnp.zeros_like(after_ref)
+        low_ref[2 * slots :, :] = jnp.zeros((slots, 128), jnp.float32)
 
     own = me.astype(jnp.float32)
 
@@ -410,6 +470,14 @@
         to_core(sd, level).start()
 
     middle = (has_above & has_below).astype(jnp.int32)
+
+    def step_of(t):
+        j, k = (t + 3) // 4 - 1, (t + 3) % 4
+        column = (k == 0) & (j < CHIP_Z - 1) | (t == 0)
+        slanted = (k == 3) & (j >= 1) | (t == 4 * CHIP_Z + 1)
+        position = jnp.where(t == 0, 0, jnp.where(column, j + 1, jnp.where(slanted, j - 1, j)))
+        seg = jnp.where(column, s, jnp.where(slanted, sd, jnp.where(k == 1, sx, sy)))
+        return column | slanted | (k == 1) | (k == 2), seg * CHIP_Z + level_of(position)
 
     @pl.loop(0, 4 * CHIP_Z + 2)
     def _(t):
@@ -429,30 +497,29 @@
 
         pl.when((k == 2) & (j >= 1) & (j < CHIP_Z))(lambda: diagonal(level_of(j - 1)))
         pl.when(t == 4 * CHIP_Z + 1)(lambda: diagonal(level_of(CHIP_Z - 1)))
-        column = (k == 0) & (j < CHIP_Z - 1) | (t == 0)
-        slanted = (k == 3) & (j >= 1) | (t == 4 * CHIP_Z + 1)
-        position = jnp.where(t == 0, 0, jnp.where(column, j + 1, jnp.where(slanted, j - 1, j)))
-        seg = jnp.where(column, s, jnp.where(slanted, sd, jnp.where(k == 1, sx, sy)))
-        chip = seg * CHIP_Z + level_of(position)
-
-        @pl.when(column | slanted | (k == 1) | (k == 2))
+        active, chip = step_of(t)
+
+        @pl.when(active)
         def _():
             from_core(chip).wait_recv()
             gathered, octants = [], []
             for c in range(2):
                 block = held_ref[chip * 2 + c]
                 mask = jnp.where(block[OWNERS:, :] == own, 1.0, 0.0)
-                held, octant = chosen_children(block[:OWNERS, :], keys_of(mask, earlier_ref[...]), WIDTH // 2)
+                held, octant = chosen_children(block[:OWNERS, :], keys_of(mask, table_ref[EARLIER : EARLIER + 256, :256]), WIDTH // 2)
                 gathered.append(held)
                 octants.append(octant)
             mass, face = masses(
-                jnp.concatenate(gathered, axis=1), jnp.concatenate(octants, axis=1), a1_ref, a2_ref, a3_ref, ad_ref
+                jnp.concatenate(gathered, axis=1), jnp.concatenate(octants, axis=1), table_ref
             )
             lanes = pl.ds(pl.multiple_of(chip * WIDTH, WIDTH), WIDTH)
             mass_ref[:, lanes] = mass
             face_ref[:, lanes] = face
-            pl.when(has_next)(lambda: to_next(chip).start())
-            pl.when(has_prev)(lambda: to_prev(chip).start())
+            low_ref[pl.ds(pl.multiple_of(slots + chip * WIDTH, WIDTH), WIDTH), :] = face[:128].T
+            pl.when(t >= DELAY)(lambda: send_faces(chip))
+
+        waiting, old = step_of(jnp.maximum(t - DELAY, 0))
+        pl.when((t >= DELAY) & (t < 2 * DELAY) & waiting)(lambda: send_faces(old))
 
     @pl.loop(0, CHIP_Z)
     def _(level):
@@ -469,53 +536,55 @@
 
         @pl.when(has_next)
         def _():
-            to_next(chip).wait_send()
-            remote(
-                piece(face_ref, chip), piece(after_ref, chip), send_next.at[chip], recv_after.at[chip], next_one
-            ).wait_recv()
+            for copy in to_next(chip):
+                copy.wait_send()
+            for copy in from_next(chip):
+                copy.wait_recv()
 
         @pl.when(has_prev)
         def _():
-            to_prev(chip).wait_send()
-            remote(
-                piece(face_ref, chip), piece(before_ref, chip), send_prev.at[chip], recv_before.at[chip], prev_one
-            ).wait_recv()
-
-
-def gather_and_compute(nodes, marks, owners, pick, tables, cap):
+            for copy in to_prev(chip):
+                copy.wait_send()
+            for copy in from_prev(chip):
+                copy.wait_recv()
+
+
+def gather_and_compute(nodes, marks, owners, tables, cap):
     devices = 8 * CHIP_Z
     slots = devices * cap
     vmem = pl.BlockSpec(memory_space=pltpu.VMEM)
-    faces = jax.ShapeDtypeStruct((152, slots), jnp.float32)
+    faces = jax.ShapeDtypeStruct((FACES, slots), jnp.float32)
+    low = jax.ShapeDtypeStruct((3 * slots, 128), jnp.float32)
+    strips = jax.ShapeDtypeStruct((STRIP, slots), jnp.float32)
     dma = pltpu.SemaphoreType.DMA
     chips = 4 * CHIP_Z
     return pl.pallas_call(
         gather_kernel,
-        in_specs=[vmem] * (4 + len(tables)),
-        out_specs=[vmem] * 4,
-        out_shape=[jax.ShapeDtypeStruct((125, slots), jnp.float32), faces, faces, faces],
+        in_specs=[vmem] * 4,
+        out_specs=[vmem] * 5,
+        out_shape=[jax.ShapeDtypeStruct((125, slots), jnp.float32), faces, low, strips, strips],
         scratch_shapes=[pltpu.VMEM((devices, OWNERS + 8, owners.shape[1]), jnp.float32)]
         + [dma((CHIP_Z,))] * 6
-        + [dma((chips,))] * 3
+        + [dma((chips,))] * 5
         + [dma((CHIP_Z,))] * 5
-        + [dma((chips,))] * 3,
+        + [dma((chips,))] * 5,
         compiler_params=pltpu.CompilerParams(
             collective_id=0, has_side_effects=True, vmem_limit_bytes=48 * 1024 * 1024
         ),
         name="gather_and_compute",
-    )(nodes, marks, owners, pick, *tables)
-
-
-def assemble_kernel(link_ref, before_ref, own_ref, after_ref, out_ref, low_ref, high_ref, row_low, row_high):
+    )(nodes, marks, owners, tables)
+
+
+def assemble_kernel(link_ref, low_ref, before_ref, own_ref, after_ref, out_ref, high_ref, row_low, row_high):
     slots = own_ref.shape[1]
     for part, ref in enumerate((before_ref, own_ref, after_ref)):
 
-        @pl.loop(0, slots // 128)
+        @pl.loop(0, slots // 512)
         def _(number):
-            start = pl.multiple_of(number * 128, 128)
-            rows = pl.ds(pl.multiple_of(part * slots + number * 128, 128), 128)
-            low_ref[rows, :] = ref[0:128, pl.ds(start, 128)].T
-            high_ref[rows, :] = ref[24:152, pl.ds(start, 128)].T
+            for k in range(4):
+                start = pl.multiple_of(number * 512 + k * 128, 128)
+                rows = pl.ds(pl.multiple_of(part * slots + number * 512 + k * 128, 128), 128)
+                high_ref[rows, :STRIP] = ref[ref.shape[0] - STRIP :, pl.ds(start, 128)].T
 
     lane = lax.broadcasted_iota(jnp.int32, (1, 128), 1)
     under = [lane < 25 * (g + 1) for g in range(4)]
@@ -536,30 +605,30 @@
                 row_high[pl.ds(inner + k, 1), :] = high_ref[pl.ds(row[4], 1), :]
 
         low = row_low[...].T
-        high = row_high[...].T
+        high = row_high[:, :STRIP].T
         fetched = [low[25 * (f ^ 1) : 25 * (f ^ 1) + 25] for f in range(4)]
-        fetched += [high[101:126], low[100:125]]
-        total = own_ref[0:150, pl.ds(start, 128)] + jnp.concatenate(fetched, axis=0)
-        out_ref[:, pl.ds(start, 128)] = total
-
-
-def assemble(link, before, own, after):
+        fetched += [high[0:25], low[100:125]]
+        lanes = pl.ds(start, 128)
+        own = [own_ref[0:125, lanes], own_ref[128:153, lanes]]
+        out_ref[:, lanes] = jnp.concatenate(own, axis=0) + jnp.concatenate(fetched, axis=0)
+
+
+def assemble(link, low, before, own, after):
     slots = own.shape[1]
     vmem = pl.BlockSpec(memory_space=pltpu.VMEM)
     return pl.pallas_call(
         assemble_kernel,
-        in_specs=[pl.BlockSpec(memory_space=pltpu.SMEM), vmem, vmem, vmem],
+        in_specs=[pl.BlockSpec(memory_space=pltpu.SMEM), vmem, vmem, vmem, vmem],
         out_specs=vmem,
         out_shape=jax.ShapeDtypeStruct((150, slots), jnp.float32),
         scratch_shapes=[
-            pltpu.VMEM((3 * slots, 128), jnp.float32),
             pltpu.VMEM((3 * slots, 128), jnp.float32),
             pltpu.VMEM((128, 128), jnp.float32),
             pltpu.VMEM((128, 128), jnp.float32),
         ],
         compiler_params=pltpu.CompilerParams(vmem_limit_bytes=48 * 1024 * 1024),
         name="assemble",
-    )(link, before, own, after)
+    )(link, low, before, own, after)
 
 
 def body(parent_nodes, marks, child_owner, face_link):
@@ -570,9 +639,7 @@
     cap = max(2, 2 * kids // devices)
     owners = child_owner.reshape(kids // 8, 8).T.astype(jnp.float32)
     if lax.axis_size("seg") == 4 and lax.axis_size("rank") == 2 * CHIP_Z and 2 * cap == WIDTH:
-        mass, faces, before, after = gather_and_compute(
-            parent_nodes.T, marks, owners, jnp.asarray(pick, jnp.bfloat16), tables, cap
-        )
+        mass, faces, low, before, after = gather_and_compute(parent_nodes.T, marks, owners, tables, cap)
     else:
         coords = lax.dot_general(
             jnp.asarray(pick, jnp.float32),
@@ -586,7 +653,9 @@
         mass, faces = geometry(blocks, mask, tables, cap)
         before = shifted(faces, "rank", 1)
         after = shifted(faces, "rank", -1)
-    return (mass, assemble(face_link.T.reshape(-1), before, faces, after))
+        low = jnp.concatenate([before[:128].T, faces[:128].T, after[:128].T], axis=0)
+        before, after = before[128:], after[128:]
+    return (mass, assemble(face_link.T.reshape(-1), low, before, faces, after))
 
 
 def solution(mesh):

time: 121 us -> 114 us (0.942)
  local copies, waits for them, and re-layouts: 10.5 us -> 6.26 us
  Pallas kernels: 109 us -> 105 us
    pallas_call x1, Pallas kernels: 37.4 us -> 31.6 us  [assemble(): pl.pallas_call(assemble_kernel, in_specs=[pl.BlockSpec(memory_space=pltpu...]
    unnamed x17 -> x7, local copies, waits for them, and re-layouts: 9.37 us -> 5.15 us
    pallas_call x1, Pallas kernels: 71.2 us -> 73.4 us  [gather_and_compute(): pl.pallas_call(gather_kernel, in_specs=[vmem] * 4, out_specs=[vmem] * 5,...]
where the time goes in v4:
time: 114 us; the launch traced here: 113 us
  Pallas kernels  105 us (92%)
  local copies, waits for them, and re-layouts  6.26 us (5%)
    pallas_call x1, Pallas kernels, gather_and_compute(): pl.pallas_call(gather_kernel, in_specs=[vmem] * 4, out_specs=[vmem] * 5,...  73.4 us
    pallas_call x1, Pallas kernels, assemble(): pl.pallas_call(assemble_kernel, in_specs=[pl.BlockSpec(memory_space=pltpu...  31.6 us
    unnamed x7, local copies, waits for them, and re-layouts  5.15 us

profile of v4, /device:TPU:1, one launch (start us, length us, event | category | flops | bytes accessed | tf_op | source)
XLA Modules:
  0.0 112.7 jit_solution(12495513894619093165)
XLA Ops:
  0.6 0.7 convert_reduce_fusion
  1.4 1.0 reshape.9.link_ref
  2.3 0.1 convert_element_type.8
  2.4 0.1 copy.7
  2.5 0.0 copy-start.1
  2.5 1.4 %copy-done.1 = bf16[2040,384]{1,0:T(8,128)(2,1)S(1)} copy-done((bf16[2040,384]{1,0:T(8,128)(2,1)S(1)}, bf16[2040,384]{1,0:T(8,128)(2,1)}, u32[]{:S(2)}) %copy-start.1) | copy-done | bytes 1566744
  3.9 0.0 copy-start.2
  3.9 0.7 copy-done.2
  4.6 73.4 %gather_and_compute.1 = (f32[125,4096]{1,0:T(8,128)S(1)}, f32[160,4096]{1,0:T(8,128)}, f32[12288,128]{1,0:T(8,128)}, f32[32,4096]{1,0:T(8,128)S(1)}, f32[32,4096]{1,0:T(8,128)S(1)}) custom-call(f32[375,2560]{1,0:T(8,128)} %bitcast.4, s32[1,256]{1,0:T(1,128)S(1)} %copy-done.2, f32[8,256]{1,0:T(8,128)S(1)} %bitcast.3, bf16[2040,384]{1,0:T(8,128)(2,1)S(1)} %copy-done.1), custom_call_target="tpu_custom_call" | custom-call | tf_op jit(solution)/shard_map/gather_and_compute/pallas_call | solution.py:561
  78.0 0.0 copy-start
  78.0 1.7 %copy-done = f32[160,4096]{1,0:T(8,128)S(1)} copy-done((f32[160,4096]{1,0:T(8,128)S(1)}, f32[160,4096]{1,0:T(8,128)}, u32[]{:S(2)}) %copy-start) | copy-done | bytes 2621464
  79.7 31.6 %assemble.1 = f32[150,4096]{1,0:T(8,128)} custom-call(s32[24576]{0:T(1024)S(1)} %reshape.9.link_ref, f32[12288,128]{1,0:T(8,128)} %get-tuple-element.8.low_ref, f32[32,4096]{1,0:T(8,128)S(1)} %get-tuple-element.9.before_ref, f32[160,4096]{1,0:T(8,128)S(1)} %copy-done, f32[32,4096]{1,0:T(8,128)S(1)} %get-tuple-element.11.after_ref), custom_call_target="tpu_custom_call" | custom-call | tf_op jit(solution)/shard_map/assemble/pallas_call | solution.py:619
  111.3 1.3 %copy.9 = f32[125,4096]{1,0:T(8,128)} copy(f32[125,4096]{1,0:T(8,128)S(1)} %get-tuple-element.14) | data formatting | bytes 4096000
Async XLA Ops:
  2.5 1.4 %copy-start.1 = (bf16[2040,384]{1,0:T(8,128)(2,1)S(1)}, bf16[2040,384]{1,0:T(8,128)(2,1)}, u32[]{:S(2)}) copy-start(bf16[2040,384]{1,0:T(8,128)(2,1)} %constant.2.clone.table_ref) | copy-start | bytes 4700164
  3.9 0.7 copy-start.2
  78.0 1.7 %copy-start = (f32[160,4096]{1,0:T(8,128)S(1)}, f32[160,4096]{1,0:T(8,128)}, u32[]{:S(2)}) copy-start(f32[160,4096]{1,0:T(8,128)} %get-tuple-element.10.own_ref) | copy-start | bytes 7864324

commit v5 on v4

--- a/solution.py
+++ b/solution.py
@@ -278,7 +278,7 @@
 
 
 MESH = pl.DeviceIdType.MESH
-DELAY = 5
+DELAY = 2
 CHIP_Z = 4
 
 
@@ -589,28 +589,25 @@
     lane = lax.broadcasted_iota(jnp.int32, (1, 128), 1)
     under = [lane < 25 * (g + 1) for g in range(4)]
 
-    @pl.loop(0, slots // 128)
+    @pl.loop(0, slots // 256)
     def _(number):
-        start = pl.multiple_of(number * 128, 128)
-
-        @pl.loop(0, 128, step=16)
-        def _(inner):
-            for k in range(16):
-                u = start + inner + k
-                row = [link_ref[f * slots + u] for f in range(6)]
+        for b in range(2):
+            start = pl.multiple_of(number * 256 + b * 128, 128)
+            for k in range(128):
+                row = [link_ref[start + (f * slots + k)] for f in range(6)]
                 value = low_ref[pl.ds(row[5], 1), :]
                 for g in (3, 2, 1, 0):
                     value = jnp.where(under[g], low_ref[pl.ds(row[g ^ 1], 1), :], value)
-                row_low[pl.ds(inner + k, 1), :] = value
-                row_high[pl.ds(inner + k, 1), :] = high_ref[pl.ds(row[4], 1), :]
-
-        low = row_low[...].T
-        high = row_high[:, :STRIP].T
-        fetched = [low[25 * (f ^ 1) : 25 * (f ^ 1) + 25] for f in range(4)]
-        fetched += [high[0:25], low[100:125]]
-        lanes = pl.ds(start, 128)
-        own = [own_ref[0:125, lanes], own_ref[128:153, lanes]]
-        out_ref[:, lanes] = jnp.concatenate(own, axis=0) + jnp.concatenate(fetched, axis=0)
+                row_low[b, k : k + 1, :] = value
+                row_high[b, k : k + 1, :] = high_ref[pl.ds(row[4], 1), :]
+
+            low = row_low[b].T
+            high = row_high[b, :, :STRIP].T
+            fetched = [low[25 * (f ^ 1) : 25 * (f ^ 1) + 25] for f in range(4)]
+            fetched += [high[0:25], low[100:125]]
+            lanes = pl.ds(start, 128)
+            own = [own_ref[0:125, lanes], own_ref[128:153, lanes]]
+            out_ref[:, lanes] = jnp.concatenate(own, axis=0) + jnp.concatenate(fetched, axis=0)
 
 
 def assemble(link, low, before, own, after):
@@ -623,8 +620,8 @@
         out_shape=jax.ShapeDtypeStruct((150, slots), jnp.float32),
         scratch_shapes=[
             pltpu.VMEM((3 * slots, 128), jnp.float32),
-            pltpu.VMEM((128, 128), jnp.float32),
-            pltpu.VMEM((128, 128), jnp.float32),
+            pltpu.VMEM((2, 128, 128), jnp.float32),
+            pltpu.VMEM((2, 128, 128), jnp.float32),
         ],
         compiler_params=pltpu.CompilerParams(vmem_limit_bytes=48 * 1024 * 1024),
         name="assemble",

time: 114 us -> 110 us (0.965)
  Pallas kernels: 105 us -> 102 us
    pallas_call x1, Pallas kernels: 31.6 us -> 28.6 us  [assemble(): pl.pallas_call(assemble_kernel, in_specs=[pl.BlockSpec(memory_space=pltpu...]
where the time goes in v5:
time: 110 us
  Pallas kernels  102 us (93%)
  local copies, waits for them, and re-layouts  6.26 us (6%)
    pallas_call x1, Pallas kernels, gather_and_compute(): pl.pallas_call(gather_kernel, in_specs=[vmem] * 4, out_specs=[vmem] * 5,...  73.3 us
    pallas_call x1, Pallas kernels, assemble(): pl.pallas_call(assemble_kernel, in_specs=[pl.BlockSpec(memory_space=pltpu...  28.6 us
    unnamed x7, local copies, waits for them, and re-layouts  5.15 us

profile of v5, /device:TPU:1, one launch (start us, length us, event | category | flops | bytes accessed | tf_op | source)
XLA Modules:
  0.0 109.6 jit_solution(8799127161726844050)
XLA Ops:
  0.6 0.7 convert_reduce_fusion
  1.4 1.0 reshape.9.link_ref
  2.3 0.1 convert_element_type.8
  2.4 0.1 copy.7
  2.5 0.0 copy-start.1
  2.5 1.4 %copy-done.1 = bf16[2040,384]{1,0:T(8,128)(2,1)S(1)} copy-done((bf16[2040,384]{1,0:T(8,128)(2,1)S(1)}, bf16[2040,384]{1,0:T(8,128)(2,1)}, u32[]{:S(2)}) %copy-start.1) | copy-done | bytes 1566744
  3.9 0.0 copy-start.2
  3.9 0.7 copy-done.2
  4.6 73.3 %gather_and_compute.1 = (f32[125,4096]{1,0:T(8,128)S(1)}, f32[160,4096]{1,0:T(8,128)}, f32[12288,128]{1,0:T(8,128)}, f32[32,4096]{1,0:T(8,128)S(1)}, f32[32,4096]{1,0:T(8,128)S(1)}) custom-call(f32[375,2560]{1,0:T(8,128)} %bitcast.4, s32[1,256]{1,0:T(1,128)S(1)} %copy-done.2, f32[8,256]{1,0:T(8,128)S(1)} %bitcast.3, bf16[2040,384]{1,0:T(8,128)(2,1)S(1)} %copy-done.1), custom_call_target="tpu_custom_call" | custom-call | tf_op jit(solution)/shard_map/gather_and_compute/pallas_call | solution.py:561
  77.9 0.0 copy-start
  77.9 1.7 %copy-done = f32[160,4096]{1,0:T(8,128)S(1)} copy-done((f32[160,4096]{1,0:T(8,128)S(1)}, f32[160,4096]{1,0:T(8,128)}, u32[]{:S(2)}) %copy-start) | copy-done | bytes 2621464
  79.6 28.6 %assemble.1 = f32[150,4096]{1,0:T(8,128)} custom-call(s32[24576]{0:T(1024)S(1)} %reshape.9.link_ref, f32[12288,128]{1,0:T(8,128)} %get-tuple-element.8.low_ref, f32[32,4096]{1,0:T(8,128)S(1)} %get-tuple-element.9.before_ref, f32[160,4096]{1,0:T(8,128)S(1)} %copy-done, f32[32,4096]{1,0:T(8,128)S(1)} %get-tuple-element.11.after_ref), custom_call_target="tpu_custom_call" | custom-call | tf_op jit(solution)/shard_map/assemble/pallas_call | solution.py:616
  108.3 1.3 %copy.9 = f32[125,4096]{1,0:T(8,128)} copy(f32[125,4096]{1,0:T(8,128)S(1)} %get-tuple-element.14) | data formatting | bytes 4096000
Async XLA Ops:
  2.5 1.4 %copy-start.1 = (bf16[2040,384]{1,0:T(8,128)(2,1)S(1)}, bf16[2040,384]{1,0:T(8,128)(2,1)}, u32[]{:S(2)}) copy-start(bf16[2040,384]{1,0:T(8,128)(2,1)} %constant.2.clone.table_ref) | copy-start | bytes 4700164
  3.9 0.7 copy-start.2
  77.9 1.7 %copy-start = (f32[160,4096]{1,0:T(8,128)S(1)}, f32[160,4096]{1,0:T(8,128)}, u32[]{:S(2)}) copy-start(f32[160,4096]{1,0:T(8,128)} %get-tuple-element.10.own_ref) | copy-start | bytes 7864324
